TPU v7x, 512 devices: a whole 4x4x16 slice. The times are simulated.
512 devices in a mesh: lat: 32 (over z, y_lo), lon: 16 (over y_hi, x, core).
Axes of the slice: x: 4, y: 4 (y_hi: 2, y_lo: 2; y = y_hi * 2 + y_lo), z: 16, core: 2. Of those that a mesh axis runs over, the one named last changes fastest.
Arguments:
- grid_state: bfloat16 [1, 128, 1024, 1024], P(None, 'lat', 'lon'), may hold values from -45 to 45
- stencil_one: float32 [2, 3, 1024], replicated, may hold values from -1.5 to 1.5
- stencil_two: float32 [2, 3, 1024], replicated, may hold values from -1.5 to 1.5
- norm_gain: float32 [1024], replicated, may hold values from 0.5 to 1.5
- query_weight: bfloat16 [1024, 1024], replicated, may hold values from -0.125 to 0.125
- key_value_weight: bfloat16 [1024, 512], replicated, may hold values from -3.125 to 3.125
Outputs:
- mixed_field: bfloat16 [1, 128, 1024, 1024], P(None, 'lat', 'lon')
- attended: bfloat16 [1, 128, 1024, 1024], P(None, 'lat', 'lon')
All inputs are finite; a program needn't handle non-finite values.
Results may differ from a plain program's by a relative error of at most 0.035.
Values may be sent and summed in bfloat16 or wider, within the bound.
No kernel may reach another device: no remote copies, remote signals or barrier semaphores. Data moves between devices by JAX's collectives and lax.ppermute only.
A program may use at most 64 MiB of HBM per device.

v0:
```python
import math

import jax
import jax.numpy as jnp
from jax import lax
from jax.sharding import PartitionSpec as P

HEADS = 16
KV_HEADS = 4
HEAD_DIM = 64


def extended_2(cells, sides, width, closed):
    for axis, dim in sides:
        count = lax.axis_size(axis)
        ends = count if closed else count - 1
        head = lax.slice_in_dim(cells, 0, width, axis=dim)
        tail = lax.slice_in_dim(cells, cells.shape[dim] - width, cells.shape[dim], axis=dim)
        cells = jnp.concatenate(
            [
                lax.ppermute(tail, axis, [(i, (i + 1) % count) for i in range(ends)]),
                cells,
                lax.ppermute(head, axis, [((i + 1) % count, i) for i in range(ends)]),
            ],
            axis=dim,
        )
    return cells


def from_partner(x, axis, distance):
    return lax.ppermute(x, axis, [(i, i ^ 1 << distance) for i in range(lax.axis_size(axis))])


def band_weights(first_row, row_count, nlat_total):
    positions = (jnp.arange(row_count, dtype=jnp.int32) + first_row).astype(jnp.float32)
    return jnp.abs(jnp.sin(jnp.pi * (positions + 0.5) / nlat_total))


def apply_stencil(extended, weights, row_weights):
    scaled = extended.astype(jnp.float32) * row_weights[None, :, None, None]
    column_count = extended.shape[2] - 2
    running = jnp.zeros_like(scaled[:, 1:-1, 1:-1])
    for offset in range(3):
        centre = scaled[:, 1:-1, offset : offset + column_count]
        beside = (
            scaled[:, :-2, offset : offset + column_count]
            + scaled[:, 2:, offset : offset + column_count]
        )
        running = running + weights[0, offset] * centre + weights[1, offset] * beside
    return (extended[:, 1:-1, 1:-1].astype(jnp.float32) + running).astype(jnp.bfloat16)


def place_poles(band_rows, mirrored, margin):
    band_index = lax.axis_index("lat")
    last_band = lax.axis_size("lat") - 1
    upper_rim = jnp.where(band_index == 0, mirrored[:, :margin][:, ::-1], band_rows[:, :margin])
    lower_rim = jnp.where(
        band_index == last_band, mirrored[:, margin:][:, ::-1], band_rows[:, -margin:]
    )
    return jnp.concatenate([upper_rim, band_rows[:, margin:-margin], lower_rim], axis=1)


def extend_once(layer_input):
    band_rows = extended_2(layer_input, (("lat", 1),), 1, False)
    polar_rows = jnp.concatenate([layer_input[:, :1], layer_input[:, -1:]], axis=1)
    mirrored = from_partner(polar_rows, "lon", lax.axis_size("lon").bit_length() - 2)
    band_rows = place_poles(band_rows, mirrored, 1)
    return extended_2(band_rows, (("lon", 2),), 1, True)


def local(grid_state, stencil_one, stencil_two, norm_gain, query_weight, key_value_weight):
    level_count, band_count, lon_count, channels = grid_state.shape
    circles = level_count * band_count
    nlat_total = band_count * lax.axis_size("lat")
    band_start = lax.axis_index("lat") * band_count
    row_weights = band_weights(band_start - 1, band_count + 2, nlat_total)
    after_one = apply_stencil(extend_once(grid_state), stencil_one, row_weights)
    mixed_field = apply_stencil(extend_once(after_one), stencil_two, row_weights)
    flattened = mixed_field.reshape(circles * lon_count, channels).astype(jnp.float32)
    mean_square = jnp.mean(flattened * flattened, axis=-1, keepdims=True)
    normed = (flattened * lax.rsqrt(mean_square + 1e-06) * norm_gain).astype(jnp.bfloat16)
    queries = jnp.dot(normed, query_weight, preferred_element_type=jnp.float32).astype(jnp.bfloat16)
    key_values = jnp.dot(normed, key_value_weight, preferred_element_type=jnp.float32).astype(
        jnp.bfloat16
    )
    key_width = KV_HEADS * HEAD_DIM
    queries = queries.reshape(circles, lon_count, channels)
    key_rows = key_values[:, :key_width].reshape(circles, lon_count, key_width)
    value_rows = key_values[:, key_width:].reshape(circles, lon_count, key_width)
    groups = HEADS // KV_HEADS
    grouped_queries = queries.reshape(circles, lon_count, KV_HEADS, groups, HEAD_DIM)
    start_peak = jnp.full((circles, KV_HEADS, groups, lon_count), -jnp.inf, jnp.float32)
    start_sum = jnp.zeros((circles, KV_HEADS, groups, lon_count), jnp.float32)
    start_acc = jnp.zeros((circles, KV_HEADS, groups, lon_count, HEAD_DIM), jnp.float32)
    key_block = lax.all_gather(key_rows, "lon", axis=1, tiled=True)
    value_block = lax.all_gather(value_rows, "lon", axis=1, tiled=True)
    block_cols = key_block.shape[1]
    key_block = key_block.reshape(circles, block_cols, KV_HEADS, HEAD_DIM)
    value_block = value_block.reshape(circles, block_cols, KV_HEADS, HEAD_DIM)

    def one_band(packed):
        row_peak, denominator, running, query_band, key_band, value_band = packed
        scores = jnp.einsum(
            "wkgd,pkd->kgwp", query_band, key_band, preferred_element_type=jnp.float32
        ) / math.sqrt(HEAD_DIM)
        new_peak = jnp.maximum(row_peak, jnp.max(scores, axis=-1))
        factor = jnp.exp(row_peak - new_peak)
        exponent = jnp.exp(scores - new_peak[..., None])
        denominator = denominator * factor + jnp.sum(exponent, axis=-1)
        update = jnp.einsum(
            "kgwp,pkd->kgwd",
            exponent.astype(jnp.bfloat16),
            value_band,
            preferred_element_type=jnp.float32,
        )
        running = running * factor[..., None] + update
        return (new_peak, denominator, running)

    row_peak, denominator, running = lax.map(
        one_band, (start_peak, start_sum, start_acc, grouped_queries, key_block, value_block)
    )
    mixed = running / denominator[..., None]
    attended = (
        jnp.transpose(mixed, (0, 3, 1, 2, 4))
        .reshape(circles, lon_count, channels)
        .astype(jnp.bfloat16)
    )
    return (mixed_field, attended.reshape(level_count, band_count, lon_count, channels))


def solution(mesh):
    in_specs = (P(None, "lat", "lon", None), P(), P(), P(), P(), P())
    out_specs = (P(None, "lat", "lon", None), P(None, "lat", "lon", None))
    return jax.shard_map(local, mesh=mesh, in_specs=in_specs, out_specs=out_specs, check_vma=False)
```

profile of v0, /device:TPU:1, one launch (start us, length us, event | category | flops | bytes accessed | tf_op | source)
XLA Modules:
  0.0 243.3 jit_solution(15090964813577795990)
XLA Ops:
  7.2 1.2 fusion.49
  8.4 5.7 %collective-permute-start = (bf16[1,2,64,1024]{3,2,1,0:T(8,128)(2,1)S(1)}, bf16[1,2,64,1024]{3,2,1,0:T(8,128)(2,1)S(1)}, u32[]{:S(2)}, u32[]{:S(2)}) collective-permute-start(bf16[1,2,64,1024]{3,2,1,0:T(8,128)(2,1)S(1)} %pad_maximum_fusion), channel_id=1, source_target_pairs={{0,8},{1,9},{2,10},{3,11},{4,12},{5,13},{6,14},{7,15},{8,0},{9,1},... | collective-permute-start | bytes 786440 | tf_op jit(solution)/shard_map/ppermute | solution.py:31
  14.1 2.3 collective-permute-start.1
  16.4 1.3 collective-permute-start.2
  17.7 0.8 fusion.52
  18.5 1.1 collective-permute-done.1
  19.6 3.8 %collective-permute-done.2 = bf16[1,1,64,1024]{3,2,1,0:T(8,128)(2,1)} collective-permute-done((bf16[1,1,64,1024]{3,2,1,0:T(8,128)(2,1)S(1)}, bf16[1,1,64,1024]{3,2,1,0:T(8,128)(2,1)}, u32[]{:S(2)}, u32[]{:S(2)}) %collective-permute-start.2) | collective-permute-done | bytes 131104 | tf_op jit(solution)/shard_map/ppermute | solution.py:23
  23.4 0.9 slice_select_fusion.3
  24.4 5.9 %collective-permute-start.3 = (bf16[1,6,1,1024]{3,2,1,0:T(2,128)(2,1)S(1)}, bf16[1,6,1,1024]{3,2,1,0:T(2,128)(2,1)S(1)}, u32[]{:S(2)}, u32[]{:S(2)}) collective-permute-start(bf16[1,6,1,1024]{3,2,1,0:T(2,128)(2,1)S(1)} %get-tuple-element.61), channel_id=1, source_target_pairs={{0,1},{1,2},{2,3},{3,4},{4,5},{5,6},{6,7},{7,8},{8,9},{9,10},{10,1... | collective-permute-start | bytes 36872 | tf_op jit(solution)/shard_map/ppermute | solution.py:21
  30.3 2.5 %collective-permute-start.4 = (bf16[1,6,1,1024]{3,2,1,0:T(2,128)(2,1)S(1)}, bf16[1,6,1,1024]{3,2,1,0:T(2,128)(2,1)S(1)}, u32[]{:S(2)}, u32[]{:S(2)}) collective-permute-start(bf16[1,6,1,1024]{3,2,1,0:T(2,128)(2,1)S(1)} %get-tuple-element.62), channel_id=1, source_target_pairs={{1,0},{2,1},{3,2},{4,3},{5,4},{6,5},{7,6},{8,7},{9,8},{10,9},{11,1... | collective-permute-start | bytes 36872 | tf_op jit(solution)/shard_map/ppermute | solution.py:23
  32.8 2.9 %collective-permute-done.4 = bf16[1,6,1,1024]{3,2,1,0:T(2,128)(2,1)S(1)} collective-permute-done((bf16[1,6,1,1024]{3,2,1,0:T(2,128)(2,1)S(1)}, bf16[1,6,1,1024]{3,2,1,0:T(2,128)(2,1)S(1)}, u32[]{:S(2)}, u32[]{:S(2)}) %collective-permute-start.4) | collective-permute-done | bytes 12320 | tf_op jit(solution)/shard_map/ppermute | solution.py:23
  35.7 0.4 convert_multiply_fusion.1
  36.1 0.8 fusion.37
  36.9 1.9 collective-permute-start.5
  38.9 4.0 %collective-permute-start.6 = (bf16[1,1,64,1024]{3,2,1,0:T(8,128)(2,1)S(1)}, bf16[1,1,64,1024]{3,2,1,0:T(8,128)(2,1)S(1)}, u32[]{:S(2)}, u32[]{:S(2)}) collective-permute-start(bf16[1,1,64,1024]{3,2,1,0:T(8,128)(2,1)S(1)} %get-tuple-element.63), channel_id=1, source_target_pairs={{0,16},{16,32},{32,48},{48,64},{64,80},{80,96},{96,112},{112,128},... | collective-permute-start | bytes 393224 | tf_op jit(solution)/shard_map/ppermute | solution.py:21
  42.9 1.3 collective-permute-start.7
  44.2 0.6 collective-permute-done.6
  44.8 6.1 %collective-permute-done.7 = bf16[1,1,64,1024]{3,2,1,0:T(8,128)(2,1)S(1)} collective-permute-done((bf16[1,1,64,1024]{3,2,1,0:T(8,128)(2,1)S(1)}, bf16[1,1,64,1024]{3,2,1,0:T(8,128)(2,1)S(1)}, u32[]{:S(2)}, u32[]{:S(2)}) %collective-permute-start.7) | collective-permute-done | bytes 131104 | tf_op jit(solution)/shard_map/ppermute | solution.py:23
  51.0 3.8 %collective-permute-start.8 = (bf16[1,6,1,1024]{3,2,1,0:T(2,128)(2,1)S(1)}, bf16[1,6,1,1024]{3,2,1,0:T(2,128)(2,1)S(1)}, u32[]{:S(2)}, u32[]{:S(2)}) collective-permute-start(bf16[1,6,1,1024]{3,2,1,0:T(2,128)(2,1)S(1)} %get-tuple-element.59), channel_id=1, source_target_pairs={{0,1},{1,2},{2,3},{3,4},{4,5},{5,6},{6,7},{7,8},{8,9},{9,10},{10,1... | collective-permute-start | bytes 36872 | tf_op jit(solution)/shard_map/ppermute | solution.py:21
  54.8 3.4 %collective-permute-start.9 = (bf16[1,6,1,1024]{3,2,1,0:T(2,128)(2,1)S(1)}, bf16[1,6,1,1024]{3,2,1,0:T(2,128)(2,1)S(1)}, u32[]{:S(2)}, u32[]{:S(2)}) collective-permute-start(bf16[1,6,1,1024]{3,2,1,0:T(2,128)(2,1)S(1)} %get-tuple-element.60), channel_id=1, source_target_pairs={{1,0},{2,1},{3,2},{4,3},{5,4},{6,5},{7,6},{8,7},{9,8},{10,9},{11,1... | collective-permute-start | bytes 36872 | tf_op jit(solution)/shard_map/ppermute | solution.py:23
  58.3 1.6 collective-permute-done.9
  60.0 0.4 convert_multiply_fusion
  60.3 1.2 multiply_reduce_fusion
  61.8 1.7 convolution_convert_fusion.1
  63.5 0.7 fusion.50
  64.3 0.7 all-gather.5.cloned.1.call-update
  65.0 1.5 convolution_convert_fusion
  66.5 2.5 %reshape_reshape.3 = bf16[4,64,4,4,64]{4,3,2,1,0:T(4,128)(2,1)S(1)} reshape(bf16[256,1024]{1,0:T(8,128)(2,1)} %convolution_convert_fusion) | data formatting | bytes 1048576 | tf_op jit(solution)/shard_map/reshape;reshape | solution.py:91
  69.1 70.0 %all-gather.3.cloned.1.call-done = bf16[4,1024,256]{2,1,0:T(8,128)(2,1)} async-done(((bf16[4,64,256]{2,1,0:T(8,128)(2,1)}), bf16[4,1024,256]{2,1,0:T(8,128)(2,1)}) %all-gather.3.cloned.1.call-update) | async-done | bytes 2097168 | tf_op jit(solution)/shard_map/all_gather | solution.py:95
  139.1 4.0 %copy.8 = bf16[4,1024,256]{1,2,0:T(8,128)(2,1)} copy(bf16[4,1024,256]{2,1,0:T(8,128)(2,1)} %all-gather.3.cloned.1.call-done) | data formatting | bytes 4194304 | tf_op jit(solution)/shard_map/all_gather | solution.py:95
  143.1 62.1 %all-gather.5.cloned.1.call-done = bf16[4,1024,256]{2,1,0:T(8,128)(2,1)} async-done(((bf16[4,64,256]{2,1,0:T(8,128)(2,1)}), bf16[4,1024,256]{2,1,0:T(8,128)(2,1)}) %all-gather.5.cloned.1.call-update) | async-done | bytes 2097168 | tf_op jit(solution)/shard_map/all_gather | solution.py:96
  205.2 4.0 %copy.9 = bf16[4,1024,256]{1,2,0:T(8,128)(2,1)} copy(bf16[4,1024,256]{2,1,0:T(8,128)(2,1)} %all-gather.5.cloned.1.call-done) | data formatting | bytes 4194304 | tf_op jit(solution)/shard_map/all_gather | solution.py:96
  209.2 23.0 %while.12 = (s32[]{:T(128)}, f32[4,4,4,64]{3,2,1,0:T(4,128)S(1)}, f32[4,4,4,64,64]{4,3,2,1,0:T(8,128)}, bf16[4,1024,4,64]{1,3,2,0:T(8,128)(2,1)}, bf16[4,64,4,4,...) while((s32[]{:T(128)}, f32[4,4,4,64]{3,2,1,0:T(4,128)S(1)}, ...), condition=%wide.region_4.5_spmd, body=%wide.region_1.4_spmd.sunk | while | flops 276892672 | bytes 14603861 | solution.py:119
  209.3 1.8 bitcast_reduce_fusion.2
  211.1 2.8 %fusion.64 = f32[4,4,4,64,64]{4,3,2,1,0:T(8,128)} fusion(f32[4,4,4,64,64]{4,3,2,1,0:T(8,128)} %get-tuple-element.135, s32[]{:T(128)} %get-tuple-element.133, f32[4,1024,64,4]{1,2,3,0:T(8,128)S(1)} %get-tuple-element.124, f32[4,4,64]{2,1,0:T(4,128)S(1)} %get-tuple-element.125, bf16[4,1024,4,64]{1,3,2,0:T(8,128)(2,1)} %get-tuple-element.145, ...), kind=kOutput, calls=%fused_computation.10.clone.1 | convolution fusion | flops 137428992 | bytes 5252096 | tf_op jit(solution)/shard_map/while/body/eval_jaxpr/kgwp,pkd->kgwd/dot_general | solution.py:110
  213.9 0.9 fusion.63
  215.0 1.8 bitcast_reduce_fusion.2
  216.8 2.9 %fusion.64 = f32[4,4,4,64,64]{4,3,2,1,0:T(8,128)} fusion(f32[4,4,4,64,64]{4,3,2,1,0:T(8,128)} %get-tuple-element.135, s32[]{:T(128)} %get-tuple-element.133, f32[4,1024,64,4]{1,2,3,0:T(8,128)S(1)} %get-tuple-element.124, f32[4,4,64]{2,1,0:T(4,128)S(1)} %get-tuple-element.125, bf16[4,1024,4,64]{1,3,2,0:T(8,128)(2,1)} %get-tuple-element.145, ...), kind=kOutput, calls=%fused_computation.10.clone.1 | convolution fusion | flops 137428992 | bytes 5252096 | tf_op jit(solution)/shard_map/while/body/eval_jaxpr/kgwp,pkd->kgwd/dot_general | solution.py:110
  219.7 0.9 fusion.63
  220.8 1.8 bitcast_reduce_fusion.2
  222.6 2.8 %fusion.64 = f32[4,4,4,64,64]{4,3,2,1,0:T(8,128)} fusion(f32[4,4,4,64,64]{4,3,2,1,0:T(8,128)} %get-tuple-element.135, s32[]{:T(128)} %get-tuple-element.133, f32[4,1024,64,4]{1,2,3,0:T(8,128)S(1)} %get-tuple-element.124, f32[4,4,64]{2,1,0:T(4,128)S(1)} %get-tuple-element.125, bf16[4,1024,4,64]{1,3,2,0:T(8,128)(2,1)} %get-tuple-element.145, ...), kind=kOutput, calls=%fused_computation.10.clone.1 | convolution fusion | flops 137428992 | bytes 5252096 | tf_op jit(solution)/shard_map/while/body/eval_jaxpr/kgwp,pkd->kgwd/dot_general | solution.py:110
  225.5 0.9 fusion.63
  226.5 1.8 bitcast_reduce_fusion.2
  228.4 2.9 %fusion.64 = f32[4,4,4,64,64]{4,3,2,1,0:T(8,128)} fusion(f32[4,4,4,64,64]{4,3,2,1,0:T(8,128)} %get-tuple-element.135, s32[]{:T(128)} %get-tuple-element.133, f32[4,1024,64,4]{1,2,3,0:T(8,128)S(1)} %get-tuple-element.124, f32[4,4,64]{2,1,0:T(4,128)S(1)} %get-tuple-element.125, bf16[4,1024,4,64]{1,3,2,0:T(8,128)(2,1)} %get-tuple-element.145, ...), kind=kOutput, calls=%fused_computation.10.clone.1 | convolution fusion | flops 137428992 | bytes 5252096 | tf_op jit(solution)/shard_map/while/body/eval_jaxpr/kgwp,pkd->kgwd/dot_general | solution.py:110
  231.2 0.9 fusion.63
  232.2 1.9 fusion.46
  234.1 0.8 copy.11
  234.9 1.5 convert_element_type.93
  (42 shorter events, 1.2 us)
Async XLA Ops:
  7.2 57.8 %copy-start = (bf16[1024,1024]{1,0:T(8,128)(2,1)S(1)}, bf16[1024,1024]{1,0:T(8,128)(2,1)}, u32[]{:S(2)}) copy-start(bf16[1024,1024]{1,0:T(8,128)(2,1)} %param.12) | copy-start | bytes 6291460
  7.2 17.2 %copy-start.1 = (bf16[1,4,64,1024]{3,2,1,0:T(8,128)(2,1)S(1)}, bf16[1,4,64,1024]{3,2,1,0:T(8,128)(2,1)}, u32[]{:S(2)}) copy-start(bf16[1,4,64,1024]{3,2,1,0:T(8,128)(2,1)} %param.8) | copy-start | bytes 1572868
  7.2 131.9 %all-gather.3.cloned.1.call-start = ((), (), s32[]{:S(2)}) async-start(), calls=%async_computation | async-start | bytes 2228224 | tf_op jit(solution)/shard_map/all_gather | solution.py:95
  8.4 15.0 %collective-permute-start = (bf16[1,2,64,1024]{3,2,1,0:T(8,128)(2,1)S(1)}, bf16[1,2,64,1024]{3,2,1,0:T(8,128)(2,1)S(1)}, u32[]{:S(2)}, u32[]{:S(2)}) collective-permute-start(bf16[1,2,64,1024]{3,2,1,0:T(8,128)(2,1)S(1)} %pad_maximum_fusion), channel_id=1, source_target_pairs={{0,8},{1,9},{2,10},{3,11},{4,12},{5,13},{6,14},{7,15},{8,0},{9,1},... | collective-permute-start | bytes 786440 | tf_op jit(solution)/shard_map/ppermute | solution.py:31
  14.1 5.5 %collective-permute-start.1 = (bf16[1,1,64,1024]{3,2,1,0:T(8,128)(2,1)S(1)}, bf16[1,1,64,1024]{3,2,1,0:T(8,128)(2,1)S(1)}, u32[]{:S(2)}, u32[]{:S(2)}) collective-permute-start(bf16[1,1,64,1024]{3,2,1,0:T(8,128)(2,1)S(1)} %get-tuple-element.65), channel_id=1, source_target_pairs={{0,16},{16,32},{32,48},{48,64},{64,80},{80,96},{96,112},{112,128},... | collective-permute-start | bytes 393224 | tf_op jit(solution)/shard_map/ppermute | solution.py:21
  16.4 7.0 %collective-permute-start.2 = (bf16[1,1,64,1024]{3,2,1,0:T(8,128)(2,1)S(1)}, bf16[1,1,64,1024]{3,2,1,0:T(8,128)(2,1)}, u32[]{:S(2)}, u32[]{:S(2)}) collective-permute-start(bf16[1,1,64,1024]{3,2,1,0:T(8,128)(2,1)S(1)} %get-tuple-element.66), channel_id=1, source_target_pairs={{16,0},{32,16},{48,32},{64,48},{80,64},{96,80},{112,96},{128,112},... | collective-permute-start | bytes 393224 | tf_op jit(solution)/shard_map/ppermute | solution.py:23
  24.4 8.4 %collective-permute-start.3 = (bf16[1,6,1,1024]{3,2,1,0:T(2,128)(2,1)S(1)}, bf16[1,6,1,1024]{3,2,1,0:T(2,128)(2,1)S(1)}, u32[]{:S(2)}, u32[]{:S(2)}) collective-permute-start(bf16[1,6,1,1024]{3,2,1,0:T(2,128)(2,1)S(1)} %get-tuple-element.61), channel_id=1, source_target_pairs={{0,1},{1,2},{2,3},{3,4},{4,5},{5,6},{6,7},{7,8},{8,9},{9,10},{10,1... | collective-permute-start | bytes 36872 | tf_op jit(solution)/shard_map/ppermute | solution.py:21
  30.3 5.4 %collective-permute-start.4 = (bf16[1,6,1,1024]{3,2,1,0:T(2,128)(2,1)S(1)}, bf16[1,6,1,1024]{3,2,1,0:T(2,128)(2,1)S(1)}, u32[]{:S(2)}, u32[]{:S(2)}) collective-permute-start(bf16[1,6,1,1024]{3,2,1,0:T(2,128)(2,1)S(1)} %get-tuple-element.62), channel_id=1, source_target_pairs={{1,0},{2,1},{3,2},{4,3},{5,4},{6,5},{7,6},{8,7},{9,8},{10,9},{11,1... | collective-permute-start | bytes 36872 | tf_op jit(solution)/shard_map/ppermute | solution.py:23
  36.9 21.4 %copy-start.3 = (f32[2,3,1024]{2,0,1:T(2,128)S(1)}, f32[2,3,1024]{2,0,1:T(2,128)}, u32[]{:S(2)}) copy-start(f32[2,3,1024]{2,0,1:T(2,128)} %param.10) | copy-start | bytes 73732
  36.9 14.0 %collective-permute-start.5 = (bf16[1,2,64,1024]{3,2,1,0:T(8,128)(2,1)S(1)}, bf16[1,2,64,1024]{3,2,1,0:T(8,128)(2,1)S(1)}, u32[]{:S(2)}, u32[]{:S(2)}) collective-permute-start(bf16[1,2,64,1024]{3,2,1,0:T(8,128)(2,1)S(1)} %pad_maximum_fusion.1), channel_id=1, source_target_pairs={{0,8},{1,9},{2,10},{3,11},{4,12},{5,13},{6,14},{7,15},{8,0},{9,1},... | collective-permute-start | bytes 786440 | tf_op jit(solution)/shard_map/ppermute | solution.py:31
  38.9 5.9 %collective-permute-start.6 = (bf16[1,1,64,1024]{3,2,1,0:T(8,128)(2,1)S(1)}, bf16[1,1,64,1024]{3,2,1,0:T(8,128)(2,1)S(1)}, u32[]{:S(2)}, u32[]{:S(2)}) collective-permute-start(bf16[1,1,64,1024]{3,2,1,0:T(8,128)(2,1)S(1)} %get-tuple-element.63), channel_id=1, source_target_pairs={{0,16},{16,32},{32,48},{48,64},{64,80},{80,96},{96,112},{112,128},... | collective-permute-start | bytes 393224 | tf_op jit(solution)/shard_map/ppermute | solution.py:21
  42.9 8.0 %collective-permute-start.7 = (bf16[1,1,64,1024]{3,2,1,0:T(8,128)(2,1)S(1)}, bf16[1,1,64,1024]{3,2,1,0:T(8,128)(2,1)S(1)}, u32[]{:S(2)}, u32[]{:S(2)}) collective-permute-start(bf16[1,1,64,1024]{3,2,1,0:T(8,128)(2,1)S(1)} %get-tuple-element.64), channel_id=1, source_target_pairs={{16,0},{32,16},{48,32},{64,48},{80,64},{96,80},{112,96},{128,112},... | collective-permute-start | bytes 393224 | tf_op jit(solution)/shard_map/ppermute | solution.py:23
  51.0 7.3 %collective-permute-start.8 = (bf16[1,6,1,1024]{3,2,1,0:T(2,128)(2,1)S(1)}, bf16[1,6,1,1024]{3,2,1,0:T(2,128)(2,1)S(1)}, u32[]{:S(2)}, u32[]{:S(2)}) collective-permute-start(bf16[1,6,1,1024]{3,2,1,0:T(2,128)(2,1)S(1)} %get-tuple-element.59), channel_id=1, source_target_pairs={{0,1},{1,2},{2,3},{3,4},{4,5},{5,6},{6,7},{7,8},{8,9},{9,10},{10,1... | collective-permute-start | bytes 36872 | tf_op jit(solution)/shard_map/ppermute | solution.py:21
  54.8 5.1 %collective-permute-start.9 = (bf16[1,6,1,1024]{3,2,1,0:T(2,128)(2,1)S(1)}, bf16[1,6,1,1024]{3,2,1,0:T(2,128)(2,1)S(1)}, u32[]{:S(2)}, u32[]{:S(2)}) collective-permute-start(bf16[1,6,1,1024]{3,2,1,0:T(2,128)(2,1)S(1)} %get-tuple-element.60), channel_id=1, source_target_pairs={{1,0},{2,1},{3,2},{4,3},{5,4},{6,5},{7,6},{8,7},{9,8},{10,9},{11,1... | collective-permute-start | bytes 36872 | tf_op jit(solution)/shard_map/ppermute | solution.py:23
  60.3 1.3 copy-start.4
  61.5 3.5 %copy-start.2 = (bf16[1,4,64,1024]{3,2,1,0:T(8,128)(2,1)}, bf16[1,4,64,1024]{3,2,1,0:T(8,128)(2,1)S(1)}, u32[]{:S(2)}) copy-start(bf16[1,4,64,1024]{3,2,1,0:T(8,128)(2,1)S(1)} %get-tuple-element.56) | copy-start | bytes 1572868
  64.2 141.0 %all-gather.5.cloned.1.call-start = ((), (), s32[]{:S(2)}) async-start(), calls=%async_computation.1 | async-start | bytes 2228224 | tf_op jit(solution)/shard_map/all_gather | solution.py:96
Sparse Core Ops, SparseCore 0:
  64.3 74.7 all-gather.2
  142.5 62.7 all-gather.4
where the time goes:
time: 244 us; the launch traced here: 243 us
  waiting for transfers between devices  149 us (61%)
  starting transfers between devices  32.1 us (13%)
  matrix products  21.8 us (9%)
  local copies, waits for them, and re-layouts  16 us (7%)
  between operations  14.4 us (6%)
  other arithmetic  9.74 us (4%)
    all_gather x1, waiting for transfers between devices, local(): key_block = lax.all_gather(key_rows, 'lon', axis=1, tiled=True)  70 us
    all_gather x1, waiting for transfers between devices, local(): value_block = lax.all_gather(value_rows, 'lon', axis=1, tiled=True)  62.1 us
    ppermute x4, starting transfers between devices, extended_2(): lax.ppermute(tail, axis, [(i, (i + 1) % count) for i in range(ends)])  16 us
    ppermute x4, waiting for transfers between devices, extended_2(): lax.ppermute(head, axis, [((i + 1) % count, i) for i in range(ends)])  14.4 us
    dot_general x4, matrix products, one_band(): jnp.einsum('kgwp,pkd->kgwd', exponent.astype(jnp.bfloat16), value_band, p...  11.4 us
    ppermute x4, starting transfers between devices, extended_2(): lax.ppermute(head, axis, [((i + 1) % count, i) for i in range(ends)])  8.5 us
    ppermute x2, starting transfers between devices, from_partner(): lax.ppermute(x, axis, [(i, i ^ 1 << distance) for i in range(lax.axis_siz...  7.57 us
    dot_general x4, matrix products, one_band(): jnp.einsum('wkgd,pkd->kgwp', query_band, key_band, preferred_element_type...  7.26 us
  transfers between devices with their start and end apart: 12, of which 8 were waited for; matrix products, arithmetic and copies ran while one was open for 4% of the time, Pallas kernels for 0%

commit v1 on v0

v1 whole, which is shorter than its diff:
```python
import jax
import jax.numpy as jnp
from jax import lax
from jax.experimental import pallas as pl
from jax.experimental.pallas import tpu as pltpu
from jax.sharding import PartitionSpec as P

HEADS = 16
KV_HEADS = 4
HEAD_DIM = 64
GROUPS = HEADS // KV_HEADS
QW = GROUPS * HEAD_DIM
SLOT = QW + 2 * HEAD_DIM


def meridian_pairs(bands, columns, west_north):
    half = columns // 2
    pairs = []
    for i in range(bands):
        for j in range(columns):
            if (j < half) == west_north:
                to = (i - 1, j) if i > 0 else (0, (j + half) % columns)
            else:
                to = (i + 1, j) if i < bands - 1 else (bands - 1, (j + half) % columns)
            pairs.append((i * columns + j, to[0] * columns + to[1]))
    return pairs


def extend(u):
    bands, columns = lax.axis_size("lat"), lax.axis_size("lon")
    lat, lon = lax.axis_index("lat"), lax.axis_index("lon")
    west = lon < columns // 2
    head, tail = u[:2], u[-2:]
    a = lax.ppermute(
        jnp.where(west, head, tail), ("lat", "lon"), meridian_pairs(bands, columns, True)
    )
    b = lax.ppermute(
        jnp.where(west, tail, head), ("lat", "lon"), meridian_pairs(bands, columns, False)
    )
    lower, upper = jnp.where(west, a, b), jnp.where(west, b, a)
    lower = jnp.where(lat == bands - 1, lower[::-1], lower)
    upper = jnp.where(lat == 0, upper[::-1], upper)
    rows = jnp.concatenate([upper, u, lower], axis=0)
    even = lon % 2 == 0
    left_edge, right_edge = rows[:, :2], rows[:, -2:]
    sib = lax.ppermute(
        jnp.where(even, right_edge, left_edge), "lon", [(j, j ^ 1) for j in range(columns)]
    )
    cross = lax.ppermute(
        jnp.where(even, left_edge, right_edge),
        "lon",
        [(j, (j + (1 if j % 2 else -1)) % columns) for j in range(columns)],
    )
    left, right = jnp.where(even, cross, sib), jnp.where(even, sib, cross)
    return jnp.concatenate([left, rows, right], axis=1)


def row_weights(first_row, row_count, nlat):
    positions = (jnp.arange(row_count, dtype=jnp.int32) + first_row).astype(jnp.float32)
    return jnp.abs(jnp.sin(jnp.pi * (positions + 0.5) / nlat))


def apply_stencil(extended, weights, c):
    scaled = extended.astype(jnp.float32) * c[:, None, None]
    n = extended.shape[1] - 2
    running = jnp.zeros_like(scaled[1:-1, 1:-1])
    for b in range(3):
        centre = scaled[1:-1, b : b + n]
        beside = scaled[:-2, b : b + n] + scaled[2:, b : b + n]
        running = running + weights[0, b] * centre + weights[1, b] * beside
    return (extended[1:-1, 1:-1].astype(jnp.float32) + running).astype(jnp.bfloat16)


def attention_kernel(x_ref, o_ref):
    n = x_ref.shape[0]
    k = x_ref[:, QW : QW + HEAD_DIM]
    v = x_ref[:, QW + HEAD_DIM :]
    ones = jnp.ones((n, HEAD_DIM), jnp.bfloat16)
    v_ext = jnp.concatenate([v, ones], axis=1)
    block = 256
    for i in range(n // block):
        outs = []
        for h in range(GROUPS):
            q = x_ref[i * block : (i + 1) * block, h * HEAD_DIM : (h + 1) * HEAD_DIM]
            q = q * jnp.bfloat16(HEAD_DIM**-0.5)
            s = lax.dot_general(
                q, k, (((1,), (1,)), ((), ())), preferred_element_type=jnp.float32
            )
            p = jnp.exp(s - jnp.max(s, axis=1, keepdims=True)).astype(jnp.bfloat16)
            o = jnp.dot(p, v_ext, preferred_element_type=jnp.float32)
            outs.append(o[:, :HEAD_DIM] / o[:, HEAD_DIM:])
        o_ref[i * block : (i + 1) * block, :] = jnp.concatenate(outs, axis=1).astype(jnp.bfloat16)


def attention(x):
    n = x.shape[0]
    return pl.pallas_call(
        attention_kernel,
        out_shape=jax.ShapeDtypeStruct((n, QW), jnp.bfloat16),
        in_specs=[pl.BlockSpec(memory_space=pltpu.VMEM)],
        out_specs=pl.BlockSpec(memory_space=pltpu.VMEM),
        compiler_params=pltpu.CompilerParams(vmem_limit_bytes=48 * 1024 * 1024),
        cost_estimate=pl.CostEstimate(
            flops=4 * GROUPS * n * n * HEAD_DIM,
            bytes_accessed=2 * n * (SLOT + QW),
            transcendentals=GROUPS * n * n,
        ),
        name="attention",
    )(x)


def local(grid_state, stencil_one, stencil_two, norm_gain, query_weight, key_value_weight):
    _, rows, cols, channels = grid_state.shape
    nlat = rows * lax.axis_size("lat")
    first = lax.axis_index("lat") * rows
    c = row_weights(first - 2, rows + 4, nlat)
    after_one = apply_stencil(extend(grid_state[0]), stencil_one, c)
    mixed_field = apply_stencil(after_one, stencil_two, c[1:-1])
    flat = mixed_field.reshape(rows * cols, channels).astype(jnp.float32)
    mean_square = jnp.mean(flat * flat, axis=-1, keepdims=True)
    normed = (flat * lax.rsqrt(mean_square + 1e-06) * norm_gain).astype(jnp.bfloat16)
    kw = KV_HEADS * HEAD_DIM
    weight = jnp.concatenate(
        [
            query_weight.reshape(channels, KV_HEADS, QW),
            key_value_weight[:, :kw].reshape(channels, KV_HEADS, HEAD_DIM),
            key_value_weight[:, kw:].reshape(channels, KV_HEADS, HEAD_DIM),
        ],
        axis=2,
    ).reshape(channels, KV_HEADS * SLOT)
    qkv = jnp.dot(normed, weight, preferred_element_type=jnp.float32).astype(jnp.bfloat16)
    slots = (
        qkv.reshape(rows, cols, KV_HEADS, SLOT)
        .transpose(0, 2, 1, 3)
        .reshape(rows * KV_HEADS, cols, SLOT)
    )
    circle = lax.all_to_all(slots, "lon", 0, 0, tiled=True)
    mixed = attention(circle.reshape(-1, SLOT))
    back = lax.all_to_all(mixed.reshape(-1, cols, QW), "lon", 0, 0, tiled=True)
    attended = (
        back.reshape(rows, KV_HEADS, cols, QW)
        .transpose(0, 2, 1, 3)
        .reshape(1, rows, cols, channels)
    )
    return mixed_field[None], attended


def solution(mesh):
    spec = P(None, "lat", "lon", None)
    return jax.shard_map(
        local,
        mesh=mesh,
        in_specs=(spec, P(), P(), P(), P(), P()),
        out_specs=(spec, spec),
        check_vma=False,
    )
```

time: 244 us -> 88.5 us (0.36)
  waiting for transfers between devices: 149 us -> 2.82 us
  blocking collectives: 0 us -> 36.9 us
  matrix products: 21.8 us -> 0.98 us
  starting transfers between devices: 32.1 us -> 17.9 us
  between operations: 14.4 us -> 0.95 us
  Pallas kernels: 0 us -> 7.86 us
  local copies, waits for them, and re-layouts: 16 us -> 8.66 us
    all_gather x2 -> x0, waiting for transfers between devices: 132 us -> none  [the longest x1 70 us: local(): key_block = lax.all_gather(key_rows, 'lon', axis=1, tiled=True)]
    all_to_all x0 -> x2, blocking collectives: none -> 36.9 us  [the longest x1 22.2 us: local(): circle = lax.all_to_all(slots, 'lon', 0, 0, tiled=True)]
    dot_general x10 -> x1, matrix products: 21.8 us -> 0.98 us  [local(): jnp.dot(normed, weight, preferred_element_type=jnp.float32)]
    ppermute x10 -> x4, starting transfers between devices: 32.1 us -> 17.9 us  [the longest x1 8.42 us: extend(): lax.ppermute(jnp.where(even, right_edge, left_edge), 'lon', [(j, j ^ 1) f...]
    ppermute x10 -> x4, waiting for transfers between devices: 16.1 us -> 2.82 us  [the longest x1 2.62 us: extend(): lax.ppermute(jnp.where(even, left_edge, right_edge), 'lon', [(j, (j + (1...]
    all_gather x2 -> x0, local copies, waits for them, and re-layouts: 7.94 us -> none  [the longest x1 3.98 us: local(): key_block = lax.all_gather(key_rows, 'lon', axis=1, tiled=True)]
    pallas_call x0 -> x1, Pallas kernels: none -> 7.86 us  [attention(): pl.pallas_call(attention_kernel, out_shape=jax.ShapeDtypeStruct((n, QW),...]
    reshape x0 -> x6, local copies, waits for them, and re-layouts: none -> 7.35 us  [the longest x1 2.77 us: local(): query_weight.reshape(channels, KV_HEADS, QW)]
  transfers between devices with their start and end apart: 12 -> 4, of which waited for: 8 -> 2; matrix products, arithmetic and copies ran while one was open for 4% -> 13% of each run, Pallas kernels for 0% -> 0%
where the time goes in v1:
time: 88.5 us; the launch traced here: 88.1 us
  blocking collectives  36.9 us (42%)
  starting transfers between devices  17.9 us (20%)
  other arithmetic  12 us (14%)
  local copies, waits for them, and re-layouts  8.66 us (10%)
  Pallas kernels  7.86 us (9%)
  waiting for transfers between devices  2.82 us (3%)
  matrix products  0.98 us (1%)
  between operations  0.95 us (1%)
    all_to_all x1, blocking collectives, local(): circle = lax.all_to_all(slots, 'lon', 0, 0, tiled=True)  22.2 us
    all_to_all x1, blocking collectives, local(): back = lax.all_to_all(mixed.reshape(-1, cols, QW), 'lon', 0, 0, tiled=True)  14.7 us
    ppermute x1, starting transfers between devices, extend(): lax.ppermute(jnp.where(even, right_edge, left_edge), 'lon', [(j, j ^ 1) f...  8.42 us
    pallas_call x1, Pallas kernels, attention(): pl.pallas_call(attention_kernel, out_shape=jax.ShapeDtypeStruct((n, QW),...  7.86 us
    concatenate x1, other arithmetic, local(): jnp.concatenate([query_weight.reshape(channels, KV_HEADS, QW), key_value_...  4.62 us
    ppermute x1, starting transfers between devices, extend(): lax.ppermute(jnp.where(west, tail, head), ('lat', 'lon'), meridian_pairs(...  4.02 us
    ppermute x1, starting transfers between devices, extend(): lax.ppermute(jnp.where(west, head, tail), ('lat', 'lon'), meridian_pairs(...  3.54 us
    reshape x1, local copies, waits for them, and re-layouts, local(): query_weight.reshape(channels, KV_HEADS, QW)  2.77 us
  transfers between devices with their start and end apart: 4, of which 2 were waited for; matrix products, arithmetic and copies ran while one was open for 13% of the time, Pallas kernels for 0%

profile of v1, /device:TPU:1, one launch (start us, length us, event | category | flops | bytes accessed | tf_op | source)
XLA Modules:
  0.0 88.1 jit_solution(5155891400497329514)
XLA Ops:
  0.6 0.0 copy-start.3
  0.6 1.9 %select_bitcast_fusion.1 = (bf16[2,64,1024]{2,1,0:T(8,128)(2,1)}, bf16[2,64,1024]{2,1,0:T(8,128)(2,1)}) fusion(pred[]{:T(512)S(6)} %lt.10, bf16[1,4,64,1024]{3,2,1,0:T(8,128)(2,1)} %param.6), kind=kLoop, calls=%fused_computation.46 | loop fusion | flops 262144 | bytes 1048577 | tf_op jit(solution)/shard_map/jit(_where)/select_n | solution.py:38
  2.6 4.0 %collective-permute-start = (bf16[2,64,1024]{2,1,0:T(8,128)(2,1)}, bf16[2,64,1024]{2,1,0:T(8,128)(2,1)S(1)}, u32[]{:S(2)}, u32[]{:S(2)}) collective-permute-start(bf16[2,64,1024]{2,1,0:T(8,128)(2,1)} %get-tuple-element.13), channel_id=1, source_target_pairs={{0,16},{1,17},{2,18},{3,19},{4,20},{5,21},{6,22},{7,23},{8,0},{9,1... | collective-permute-start | bytes 786440 | tf_op jit(solution)/shard_map/ppermute | solution.py:37
  6.6 3.5 %collective-permute-start.1 = (bf16[2,64,1024]{2,1,0:T(8,128)(2,1)}, bf16[2,64,1024]{2,1,0:T(8,128)(2,1)}, u32[]{:S(2)}, u32[]{:S(2)}) collective-permute-start(bf16[2,64,1024]{2,1,0:T(8,128)(2,1)} %get-tuple-element.14), channel_id=1, source_target_pairs={{0,8},{1,9},{2,10},{3,11},{4,12},{5,13},{6,14},{7,15},{8,24},{9,25... | collective-permute-start | bytes 786440 | tf_op jit(solution)/shard_map/ppermute | solution.py:34
  10.2 0.0 copy-done.3
  10.2 0.1 fusion.25
  10.3 0.2 copy.16
  10.5 0.0 copy-start.2
  10.5 1.4 %copy.12 = bf16[1024,4,64]{2,1,0:T(4,128)(2,1)} copy(bf16[1024,4,64]{0,2,1:T(8,128)(2,1)S(1)} %bitcast.50) | data formatting | bytes 1048576 | tf_op jit(solution)/shard_map/reshape | solution.py:126
  11.9 0.2 copy.17
  12.1 1.4 %copy.13 = bf16[1024,4,64]{2,1,0:T(4,128)(2,1)} copy(bf16[1024,4,64]{0,2,1:T(8,128)(2,1)S(1)} %bitcast.51) | data formatting | bytes 1048576 | tf_op jit(solution)/shard_map/reshape | solution.py:127
  13.5 0.0 copy-done.2
  13.5 2.8 %reshape.74 = bf16[1024,4,256]{2,1,0:T(4,128)(2,1)} reshape(bf16[1024,1024]{1,0:T(8,128)(2,1)S(1)} %copy-done.2) | data formatting | bytes 4194304 | tf_op jit(solution)/shard_map/reshape | solution.py:125
  16.3 0.0 copy-start.4
  16.3 0.0 copy-start.5
  16.3 4.6 %pad_maximum_fusion = bf16[1024,4,384]{2,1,0:T(4,128)(2,1)S(1)} fusion(bf16[1024,4,64]{2,1,0:T(4,128)(2,1)} %copy.13, bf16[1024,4,64]{2,1,0:T(4,128)(2,1)} %copy.12, bf16[1024,4,256]{2,1,0:T(4,128)(2,1)} %reshape.74), kind=kLoop, calls=%fused_computation | loop fusion | flops 9437184 | bytes 6291456 | tf_op jit(solution)/shard_map/concatenate | solution.py:123
  20.9 0.0 copy-done.4
  21.0 0.0 copy-done.5
  21.0 0.0 copy-start
  21.0 0.0 collective-permute-done
  21.1 0.2 collective-permute-done.1
  21.3 1.0 %broadcast_select_fusion.1 = (bf16[2,64,1024]{2,1,0:T(8,128)(2,1)S(1)}, bf16[2,64,1024]{2,1,0:T(8,128)(2,1)S(1)}) fusion(bf16[2,64,1024]{2,1,0:T(8,128)(2,1)S(1)} %collective-permute-done, bf16[2,64,1024]{2,1,0:T(8,128)(2,1)} %collective-permute-done.1, pred[]{:T(512)S(6)} %lt.10), kind=kLoop, calls=%fused_computation.48 | loop fusion | flops 262144 | bytes 1048577 | tf_op jit(solution)/shard_map/jit(_where)/select_n | solution.py:40
  22.2 0.1 reverse_select_fusion
  22.4 0.0 copy-done
  22.4 0.1 broadcast_select_fusion.5
  22.5 8.4 %collective-permute-start.3 = (bf16[8,2,1024]{2,1,0:T(2,128)(2,1)S(1)}, bf16[8,2,1024]{2,1,0:T(2,128)(2,1)S(1)}, u32[]{:S(2)}, u32[]{:S(2)}) collective-permute-start(bf16[8,2,1024]{2,1,0:T(2,128)(2,1)S(1)} %bitcast.61), channel_id=1, source_target_pairs={{0,1},{1,0},{2,3},{3,2},{4,5},{5,4},{6,7},{7,6},{8,9},{9,8},{10,11... | collective-permute-start | bytes 98312 | tf_op jit(solution)/shard_map/ppermute | solution.py:46
  30.9 1.9 %collective-permute-start.2 = (bf16[8,2,1024]{2,1,0:T(2,128)(2,1)S(1)}, bf16[8,2,1024]{2,1,0:T(2,128)(2,1)S(1)}, u32[]{:S(2)}, u32[]{:S(2)}) collective-permute-start(bf16[8,2,1024]{2,1,0:T(2,128)(2,1)S(1)} %get-tuple-element.6), channel_id=1, source_target_pairs={{0,15},{1,2},{2,1},{3,4},{4,3},{5,6},{6,5},{7,8},{8,7},{9,10},{10,... | collective-permute-start | bytes 98312 | tf_op jit(solution)/shard_map/ppermute | solution.py:49
  32.9 0.1 slice.141
  33.0 0.6 copy.18
  33.5 0.0 collective-permute-done.3
  33.5 2.6 %collective-permute-done.2 = bf16[8,2,1024]{2,1,0:T(2,128)(2,1)S(1)} collective-permute-done((bf16[8,2,1024]{2,1,0:T(2,128)(2,1)S(1)}, bf16[8,2,1024]{2,1,0:T(2,128)(2,1)S(1)}, u32[]{:S(2)}, u32[]{:S(2)}) %collective-permute-start.2) | collective-permute-done | bytes 32800 | tf_op jit(solution)/shard_map/ppermute | solution.py:49
  36.2 0.4 pad_maximum_fusion.1
  36.5 0.5 convert_multiply_fusion
  37.0 1.9 %convert_multiply_fusion.1 = (f32[6,66,1024]{2,1,0:T(8,128)S(1)}, bf16[6,66,1024]{2,1,0:T(8,128)(2,1)S(1)}) fusion(f32[6]{0:T(128)S(1)} %slice.141, f32[8,68,1024]{2,1,0:T(8,128)S(1)} %convert_multiply_fusion, f32[1024]{0:T(1024)S(1)} %bitcast.74, f32[1024]{0:T(1024)S(1)} %bitcast.75, f32[1024]{0:T(1024)S(1)} %bitcast.71, f32[1024]{0:T(1024)S(1)} %bitcast.72, ...), kind=kLoop, calls=%fused_computation.19 | loop fusion | flops 7704576 | bytes 17866776 | tf_op jit(solution)/shard_map/mul | solution.py:64
  38.9 0.0 copy-start.6
  38.9 1.3 %fusion.10 = (f32[4,64]{1,0:T(4,128)S(1)}, bf16[4,64,1024]{2,1,0:T(8,128)(2,1)S(1)}) fusion(f32[6,66,1024]{2,1,0:T(8,128)S(1)} %get-tuple-element.4, f32[1024]{0:T(1024)S(1)} %bitcast.68, f32[1024]{0:T(1024)S(1)} %bitcast.69, f32[1024]{0:T(1024)S(1)} %bitcast.65, f32[1024]{0:T(1024)S(1)} %bitcast.66, f32[1024]{0:T(1024)S(1)} %bitcast.67, ...), kind=kLoop, calls=%fused_computation.23 | loop fusion | flops 5242624 | bytes 10511360 | tf_op jit(solution)/shard_map/reduce_sum | solution.py:120
  40.2 0.0 copy-start.1
  40.2 0.0 copy-done.6
  40.2 0.2 fusion.12
  40.4 1.0 %convolution_convert_fusion = bf16[256,1536]{1,0:T(8,128)(2,1)S(1)} fusion(bf16[256,1024]{1,0:T(8,128)(2,1)S(1)} %bitcast.54, bf16[1024,1536]{1,0:T(8,128)(2,1)S(1)} %bitcast.46), kind=kOutput, calls=%fused_computation.1 | convolution fusion | flops 805699584 | bytes 4456448 | tf_op jit(solution)/shard_map/dot_general | solution.py:131
  41.4 0.0 copy-done.1
  41.4 0.2 reshape.78
  41.6 0.1 copy.14
  41.8 22.2 %all_to_all.10 = bf16[16,64,384]{2,1,0:T(8,128)(2,1)S(1)} all-to-all(bf16[16,64,384]{2,1,0:T(8,128)(2,1)S(1)} %bitcast.48), channel_id=1, replica_groups=mesh['lat'=32,'lon'=16] {'lon'}, dimensions={0} | all-to-all | bytes 1572864 | tf_op jit(solution)/shard_map/all_to_all | solution.py:137
  64.0 7.9 %attention.1 = bf16[1024,256]{1,0:T(8,128)(2,1)S(1)} custom-call(bf16[1024,384]{1,0:T(8,128)(2,1)S(1)} %bitcast.40), custom_call_target="tpu_custom_call" | custom-call | flops 1073741824 | bytes 1310720 | tf_op jit(solution)/shard_map/attention/pallas_call | solution.py:97
  71.8 14.7 %all_to_all.11 = bf16[16,64,256]{2,1,0:T(8,128)(2,1)S(1)} all-to-all(bf16[16,64,256]{2,1,0:T(8,128)(2,1)S(1)} %bitcast.41), channel_id=1, replica_groups=mesh['lat'=32,'lon'=16] {'lon'}, dimensions={0} | all-to-all | bytes 1048576 | tf_op jit(solution)/shard_map/all_to_all | solution.py:139
  86.5 0.4 copy.20
  86.9 1.2 %reshape.83 = bf16[1,4,64,1024]{3,2,1,0:T(8,128)(2,1)} reshape(bf16[4,64,4,256]{3,2,1,0:T(4,128)(2,1)S(1)} %bitcast.53) | data formatting | bytes 1048576 | tf_op jit(solution)/shard_map/reshape | solution.py:143
  (6 shorter events, 0.1 us)
Async XLA Ops:
  0.6 9.5 %copy-start.3 = (bf16[1024,512]{1,0:T(8,128)(2,1)S(1)}, bf16[1024,512]{1,0:T(8,128)(2,1)}, u32[]{:S(2)}) copy-start(bf16[1024,512]{1,0:T(8,128)(2,1)} %param.11) | copy-start | bytes 3145732
  2.6 18.5 %collective-permute-start = (bf16[2,64,1024]{2,1,0:T(8,128)(2,1)}, bf16[2,64,1024]{2,1,0:T(8,128)(2,1)S(1)}, u32[]{:S(2)}, u32[]{:S(2)}) collective-permute-start(bf16[2,64,1024]{2,1,0:T(8,128)(2,1)} %get-tuple-element.13), channel_id=1, source_target_pairs={{0,16},{1,17},{2,18},{3,19},{4,20},{5,21},{6,22},{7,23},{8,0},{9,1... | collective-permute-start | bytes 786440 | tf_op jit(solution)/shard_map/ppermute | solution.py:37
  6.6 14.6 %collective-permute-start.1 = (bf16[2,64,1024]{2,1,0:T(8,128)(2,1)}, bf16[2,64,1024]{2,1,0:T(8,128)(2,1)}, u32[]{:S(2)}, u32[]{:S(2)}) collective-permute-start(bf16[2,64,1024]{2,1,0:T(8,128)(2,1)} %get-tuple-element.14), channel_id=1, source_target_pairs={{0,8},{1,9},{2,10},{3,11},{4,12},{5,13},{6,14},{7,15},{8,24},{9,25... | collective-permute-start | bytes 786440 | tf_op jit(solution)/shard_map/ppermute | solution.py:34
  10.5 3.1 %copy-start.2 = (bf16[1024,1024]{1,0:T(8,128)(2,1)S(1)}, bf16[1024,1024]{1,0:T(8,128)(2,1)}, u32[]{:S(2)}) copy-start(bf16[1024,1024]{1,0:T(8,128)(2,1)} %param.10) | copy-start | bytes 6291460
  16.3 4.6 %copy-start.4 = (f32[2,3,1024]{2,0,1:T(2,128)S(1)}, f32[2,3,1024]{2,0,1:T(2,128)}, u32[]{:S(2)}) copy-start(f32[2,3,1024]{2,0,1:T(2,128)} %param.7) | copy-start | bytes 73732
  16.3 4.7 %copy-start.5 = (f32[2,3,1024]{2,0,1:T(2,128)S(1)}, f32[2,3,1024]{2,0,1:T(2,128)}, u32[]{:S(2)}) copy-start(f32[2,3,1024]{2,0,1:T(2,128)} %param.8) | copy-start | bytes 73732
  21.0 1.4 %copy-start = (bf16[1,4,64,1024]{3,2,1,0:T(8,128)(2,1)S(1)}, bf16[1,4,64,1024]{3,2,1,0:T(8,128)(2,1)}, u32[]{:S(2)}) copy-start(bf16[1,4,64,1024]{3,2,1,0:T(8,128)(2,1)} %param.6) | copy-start | bytes 1572868
  22.5 11.0 %collective-permute-start.3 = (bf16[8,2,1024]{2,1,0:T(2,128)(2,1)S(1)}, bf16[8,2,1024]{2,1,0:T(2,128)(2,1)S(1)}, u32[]{:S(2)}, u32[]{:S(2)}) collective-permute-start(bf16[8,2,1024]{2,1,0:T(2,128)(2,1)S(1)} %bitcast.61), channel_id=1, source_target_pairs={{0,1},{1,0},{2,3},{3,2},{4,5},{5,4},{6,7},{7,6},{8,9},{9,8},{10,11... | collective-permute-start | bytes 98312 | tf_op jit(solution)/shard_map/ppermute | solution.py:46
  30.9 5.2 %collective-permute-start.2 = (bf16[8,2,1024]{2,1,0:T(2,128)(2,1)S(1)}, bf16[8,2,1024]{2,1,0:T(2,128)(2,1)S(1)}, u32[]{:S(2)}, u32[]{:S(2)}) collective-permute-start(bf16[8,2,1024]{2,1,0:T(2,128)(2,1)S(1)} %get-tuple-element.6), channel_id=1, source_target_pairs={{0,15},{1,2},{2,1},{3,4},{4,3},{5,6},{6,5},{7,8},{8,7},{9,10},{10,... | collective-permute-start | bytes 98312 | tf_op jit(solution)/shard_map/ppermute | solution.py:49
  38.9 1.3 %copy-start.6 = (f32[1024]{0:T(1024)S(1)}, f32[1024]{0:T(1024)}, u32[]{:S(2)}) copy-start(f32[1024]{0:T(1024)} %param.9) | copy-start | bytes 12292
  40.2 1.2 %copy-start.1 = (bf16[4,64,1024]{2,1,0:T(8,128)(2,1)}, bf16[4,64,1024]{2,1,0:T(8,128)(2,1)S(1)}, u32[]{:S(2)}) copy-start(bf16[4,64,1024]{2,1,0:T(8,128)(2,1)S(1)} %get-tuple-element.3) | copy-start | bytes 1572868

commit v2 on v1

v2 whole, which is shorter than its diff:
```python
import math

import jax
import jax.numpy as jnp
from jax import lax
from jax.experimental import pallas as pl
from jax.experimental.pallas import tpu as pltpu
from jax.sharding import PartitionSpec as P

HEADS = 16
KV_HEADS = 4
HEAD_DIM = 64
GROUPS = HEADS // KV_HEADS
QW = GROUPS * HEAD_DIM
SLOT = QW + 2 * HEAD_DIM
MARGIN = 2
LANES = 128
VMEM_LIMIT = 24 * 1024 * 1024


def meridian_pairs(bands, columns, west_north):
    half = columns // 2
    pairs = []
    for i in range(bands):
        for j in range(columns):
            if (j < half) == west_north:
                to = (i - 1, j) if i > 0 else (0, (j + half) % columns)
            else:
                to = (i + 1, j) if i < bands - 1 else (bands - 1, (j + half) % columns)
            pairs.append((i * columns + j, to[0] * columns + to[1]))
    return pairs


def row_weights(first_row, row_count, nlat):
    positions = (jnp.arange(row_count, dtype=jnp.int32) + first_row).astype(jnp.float32)
    return jnp.abs(jnp.sin(jnp.pi * (positions + 0.5) / nlat))


def add_stencil(before, here, after, raw, w_ref, lanes):
    beside = before + after
    t = [
        w_ref[0, b : b + 1, lanes] * here + w_ref[1, b : b + 1, lanes] * beside for b in range(3)
    ]
    return raw + t[1] + pltpu.roll(t[0], 1, 0) + pltpu.roll(t[2], raw.shape[0] - 1, 0)


def two_stencils(row, count, c_ref, one_ref, two_ref, lanes, store):
    raw = [row(0), row(1)]
    scaled = [raw[0] * c_ref[0], raw[1] * c_ref[1]]
    after, after_scaled = [None], [None]
    for r in range(2, count + 4):
        raw.append(row(r))
        scaled.append(raw[r] * c_ref[r])
        v = add_stencil(scaled[r - 2], scaled[r - 1], scaled[r], raw[r - 1], one_ref, lanes)
        v = v.astype(jnp.bfloat16).astype(jnp.float32)
        after.append(v)
        after_scaled.append(v * c_ref[r - 1])
        if r >= 4:
            store(
                r - 4,
                add_stencil(
                    after_scaled[r - 3],
                    after_scaled[r - 2],
                    after_scaled[r - 1],
                    after[r - 2],
                    two_ref,
                    lanes,
                ),
            )


def inner_kernel(c_ref, flag_ref, u_ref, a_ref, b_ref, one_ref, two_ref, mixed_ref, side_ref):
    rows, cols, channels = u_ref.shape
    west = flag_ref[0] == 1
    north, south = flag_ref[1], flag_ref[2]

    def chunk(n, _):
        lanes = pl.ds(pl.multiple_of(n * LANES, LANES), LANES)

        def row(r):
            if 2 <= r < rows + 2:
                main = u_ref[r - 2, :, lanes].astype(jnp.float32)
            elif r < 2:
                i = jnp.where(north == 1, 1 - r, r)
                main = jnp.where(
                    west,
                    b_ref[i, :, lanes].astype(jnp.float32),
                    a_ref[i, :, lanes].astype(jnp.float32),
                )
            else:
                i = jnp.where(south == 1, rows + 3 - r, r - rows - 2)
                main = jnp.where(
                    west,
                    a_ref[i, :, lanes].astype(jnp.float32),
                    b_ref[i, :, lanes].astype(jnp.float32),
                )
            side_ref[r, :, lanes] = main[cols - 8 :].astype(jnp.bfloat16)
            return main

        def store(r, v):
            mixed_ref[r, :, lanes] = v.astype(jnp.bfloat16)

        two_stencils(row, rows, c_ref, one_ref, two_ref, lanes, store)
        return 0

    lax.fori_loop(0, channels // LANES, chunk, 0)


def inner(c, flags, u, a, b, one, two):
    rows, cols, channels = u.shape
    vmem, smem = pl.BlockSpec(memory_space=pltpu.VMEM), pl.BlockSpec(memory_space=pltpu.SMEM)
    return pl.pallas_call(
        inner_kernel,
        out_shape=(
            jax.ShapeDtypeStruct((rows, cols, channels), jnp.bfloat16),
            jax.ShapeDtypeStruct((rows + 4, 8, channels), jnp.bfloat16),
        ),
        in_specs=[smem, smem] + [vmem] * 5,
        out_specs=(vmem, vmem),
        compiler_params=pltpu.CompilerParams(vmem_limit_bytes=VMEM_LIMIT),
        cost_estimate=pl.CostEstimate(
            flops=40 * rows * cols * channels, bytes_accessed=8 * 1024 * 1024, transcendentals=0
        ),
        name="inner",
    )(c, flags, u, a, b, one, two)


def project_kernel(
    c_ref,
    side_ref,
    edge_ref,
    inner_ref,
    one_ref,
    two_ref,
    gain_ref,
    wq,
    wkv,
    mixed_ref,
    slots_ref,
    strip,
    normed,
):
    rows, cols, channels = inner_ref.shape
    margin = edge_ref.shape[1]
    pad = jnp.zeros((8 - margin, LANES), jnp.float32)

    def chunk(n, _):
        lanes = pl.ds(pl.multiple_of(n * LANES, LANES), LANES)

        def row(r):
            return jnp.concatenate(
                [
                    side_ref[r, :, lanes].astype(jnp.float32),
                    edge_ref[r, :, lanes].astype(jnp.float32),
                    pad,
                ],
                axis=0,
            )

        def store(r, v):
            strip[r, :, lanes] = v

        two_stencils(row, rows, c_ref, one_ref, two_ref, lanes, store)
        return 0

    lax.fori_loop(0, channels // LANES, chunk, 0, unroll=2)
    place = lax.broadcasted_iota(jnp.int32, (8, channels), 0)
    for r in range(rows):
        m = inner_ref[r].astype(jnp.float32)
        m = jnp.concatenate(
            [
                jnp.where(place < MARGIN, strip[r, 8:], m[:8]),
                m[8 : cols - 8],
                jnp.where(place >= 8 - MARGIN, strip[r, :8], m[cols - 8 :]),
            ],
            axis=0,
        ).astype(jnp.bfloat16)
        mixed_ref[r] = m
        m = m.astype(jnp.float32)
        mean_square = jnp.sum(m * m, axis=1, keepdims=True) * (1.0 / channels)
        normed[r * cols : (r + 1) * cols, :] = (
            m * lax.rsqrt(mean_square + 1e-06) * gain_ref[...]
        ).astype(jnp.bfloat16)
    x = normed[...]
    kv = jnp.dot(x, wkv[...], preferred_element_type=jnp.float32).astype(jnp.bfloat16)
    kw = KV_HEADS * HEAD_DIM
    for g in range(KV_HEADS):
        q = jnp.dot(x, wq[:, g * QW : (g + 1) * QW], preferred_element_type=jnp.float32)
        q = (q * (math.log2(math.e) / math.sqrt(HEAD_DIM))).astype(jnp.bfloat16)
        at = g * HEAD_DIM
        pair = jnp.concatenate(
            [kv[:, at : at + HEAD_DIM], kv[:, kw + at : kw + at + HEAD_DIM]], axis=1
        )
        for r in range(rows):
            here = slice(r * cols, (r + 1) * cols)
            slots_ref[r * KV_HEADS + g, :, :QW] = q[here]
            slots_ref[r * KV_HEADS + g, :, QW:] = pair[here]


def project(c, side, edge, mixed, one, two, gain, wq, wkv):
    rows, cols, channels = mixed.shape
    vmem, smem = pl.BlockSpec(memory_space=pltpu.VMEM), pl.BlockSpec(memory_space=pltpu.SMEM)
    return pl.pallas_call(
        project_kernel,
        out_shape=(
            jax.ShapeDtypeStruct((rows, cols, channels), jnp.bfloat16),
            jax.ShapeDtypeStruct((rows * KV_HEADS, cols, SLOT), jnp.bfloat16),
        ),
        in_specs=[smem] + [vmem] * 8,
        out_specs=(vmem, vmem),
        scratch_shapes=[
            pltpu.VMEM((rows, 16, channels), jnp.float32),
            pltpu.VMEM((rows * cols, channels), jnp.bfloat16),
        ],
        compiler_params=pltpu.CompilerParams(vmem_limit_bytes=VMEM_LIMIT),
        cost_estimate=pl.CostEstimate(
            flops=3 * rows * cols * channels * channels,
            bytes_accessed=6 * 1024 * 1024,
            transcendentals=0,
        ),
        name="project",
    )(c, side, edge, mixed, one, two, gain, wq, wkv)


def attention_kernel(x_ref, o_ref):
    blocks, cols, _ = o_ref.shape
    n = blocks * cols
    k = x_ref[:, QW : QW + HEAD_DIM]
    ones = jnp.ones((n, HEAD_DIM), jnp.bfloat16)
    v = jnp.concatenate([x_ref[:, QW + HEAD_DIM :], ones], axis=1)
    step = n // 2
    for i in range(0, n, step):
        outs = []
        for h in range(GROUPS):
            q = x_ref[i : i + step, h * HEAD_DIM : (h + 1) * HEAD_DIM]
            s = lax.dot_general(
                q, k, (((1,), (1,)), ((), ())), preferred_element_type=jnp.float32
            )
            p = jnp.exp2(s - jnp.max(s, axis=1, keepdims=True)).astype(jnp.bfloat16)
            o = jnp.dot(p, v, preferred_element_type=jnp.float32)
            outs.append(o[:, :HEAD_DIM] / o[:, HEAD_DIM:])
        o = jnp.concatenate(outs, axis=1).astype(jnp.bfloat16)
        o_ref[i // cols : (i + step) // cols] = o.reshape(step // cols, cols, QW)
    tile = 16
    heads = [o_ref[b, :tile, :] for b in range(blocks)]
    moved = lax.broadcasted_iota(jnp.int32, (tile, QW), 0) < MARGIN
    for b in range(blocks):
        o_ref[b, :tile, :] = jnp.where(moved, heads[b - 1], heads[b])


def attention(x, blocks):
    n = x.shape[0]
    return pl.pallas_call(
        attention_kernel,
        out_shape=jax.ShapeDtypeStruct((blocks, n // blocks, QW), jnp.bfloat16),
        in_specs=[pl.BlockSpec(memory_space=pltpu.VMEM)],
        out_specs=pl.BlockSpec(memory_space=pltpu.VMEM),
        compiler_params=pltpu.CompilerParams(vmem_limit_bytes=VMEM_LIMIT),
        cost_estimate=pl.CostEstimate(
            flops=4 * GROUPS * n * n * HEAD_DIM,
            bytes_accessed=2 * n * (SLOT + QW),
            transcendentals=GROUPS * n * n,
        ),
        name="attention",
    )(x)


def gather_heads_kernel(x_ref, o_ref):
    for g in range(KV_HEADS):
        o_ref[0, :, g * QW : (g + 1) * QW] = x_ref[g]


def gather_heads(x, rows, cols, channels):
    return pl.pallas_call(
        gather_heads_kernel,
        grid=(rows,),
        out_shape=jax.ShapeDtypeStruct((rows, cols, channels), jnp.bfloat16),
        in_specs=[pl.BlockSpec((KV_HEADS, cols, QW), lambda r: (r, 0, 0))],
        out_specs=pl.BlockSpec((1, cols, channels), lambda r: (r, 0, 0)),
        compiler_params=pltpu.CompilerParams(vmem_limit_bytes=VMEM_LIMIT),
        name="gather_heads",
    )(x)


def local(grid_state, stencil_one, stencil_two, norm_gain, query_weight, key_value_weight):
    u = grid_state[0]
    rows, cols, channels = u.shape
    bands, columns = lax.axis_size("lat"), lax.axis_size("lon")
    lat, lon = lax.axis_index("lat"), lax.axis_index("lon")
    c = row_weights(lat * rows - 2, rows + 4, rows * bands)
    west = lon < columns // 2
    first, last = lat == 0, lat == bands - 1

    def towards(west_north):
        start = jnp.where(west == west_north, 0, rows - 2)
        return lax.ppermute(
            lax.dynamic_slice_in_dim(u, start, 2, axis=0),
            ("lat", "lon"),
            meridian_pairs(bands, columns, west_north),
        )

    a, b = towards(True), towards(False)

    ea, eb, eu = a[:, : 2 * MARGIN], b[:, : 2 * MARGIN], u[:, : 2 * MARGIN]
    lower, upper = jnp.where(west, ea, eb), jnp.where(west, eb, ea)
    lower = jnp.where(last, lower[::-1], lower)
    upper = jnp.where(first, upper[::-1], upper)
    edge = lax.ppermute(
        jnp.concatenate([upper, eu, lower], axis=0),
        "lon",
        [(j, (j - 1) % columns) for j in range(columns)],
    )
    flags = jnp.stack([west, first, last]).astype(jnp.int32)
    mixed_inner, side = inner(c, flags, u, a, b, stencil_one, stencil_two)
    mixed_field, slots = project(
        c,
        side,
        edge,
        mixed_inner,
        stencil_one,
        stencil_two,
        norm_gain[None],
        query_weight,
        key_value_weight,
    )
    circle = lax.all_to_all(slots, "lon", 0, 0, tiled=True)
    displaced = lax.ppermute(
        mixed_field[:, :MARGIN], "lon", [(j, (j + 1) % columns) for j in range(columns)]
    )
    mixed_field = lax.dynamic_update_slice(mixed_field, displaced, (0, 0, 0))
    circle, mixed_field = lax.optimization_barrier((circle, mixed_field))
    back = attention(circle.reshape(-1, SLOT), columns)
    back = lax.all_to_all(back, "lon", 0, 0, tiled=True)
    attended = gather_heads(back, rows, cols, channels)
    return mixed_field[None], attended[None]


def solution(mesh):
    spec = P(None, "lat", "lon", None)
    return jax.shard_map(
        local,
        mesh=mesh,
        in_specs=(spec, P(), P(), P(), P(), P()),
        out_specs=(spec, spec),
        check_vma=False,
    )
```

time: 88.5 us -> 81.1 us (0.916)
  blocking collectives: 36.9 us -> 15.3 us
  waiting for transfers between devices: 2.82 us -> 17.8 us
  other arithmetic: 12 us -> 0.21 us
  starting transfers between devices: 17.9 us -> 26 us
  Pallas kernels: 7.86 us -> 12.7 us
  local copies, waits for them, and re-layouts: 8.66 us -> 7.62 us
  matrix products: 0.98 us -> 0 us
    all_to_all x2 -> x1, blocking collectives: 36.9 us -> 15.3 us  [local(): back = lax.all_to_all(back, 'lon', 0, 0, tiled=True)]
    ppermute x4, waiting for transfers between devices: 2.82 us -> 13.2 us  [the longest x2 8.34 us: towards(): lax.ppermute(lax.dynamic_slice_in_dim(u, start, 2, axis=0), ('lat', 'lon'...]
    all_to_all x0 -> x1, starting transfers between devices: none -> 8.8 us  [local(): circle = lax.all_to_all(slots, 'lon', 0, 0, tiled=True)]
    reshape x6 -> x0, local copies, waits for them, and re-layouts: 7.35 us -> none  [the longest x1 2.77 us: local(): query_weight.reshape(channels, KV_HEADS, QW)]
    concatenate x2 -> x1, other arithmetic: 4.97 us -> 0.05 us  [local(): jnp.concatenate([upper, eu, lower], axis=0)]
    pallas_call x1 -> x4, Pallas kernels: 7.86 us -> 12.7 us  [the longest x1 5.6 us: attention(): pl.pallas_call(attention_kernel, out_shape=jax.ShapeDtypeStruct((blocks,...]
    all_to_all x0 -> x1, waiting for transfers between devices: none -> 4.59 us  [local(): circle = lax.all_to_all(slots, 'lon', 0, 0, tiled=True)]
    unnamed x17 -> x10, local copies, waits for them, and re-layouts: 1 us -> 4.15 us
  transfers between devices with their start and end apart: 4 -> 5, of which waited for: 2 -> 4; matrix products, arithmetic and copies ran while one was open for 13% -> 5% of each run, Pallas kernels for 0% -> 3%
where the time goes in v2:
time: 81.1 us; the launch traced here: 80.4 us
  starting transfers between devices  26 us (32%)
  waiting for transfers between devices  17.8 us (22%)
  blocking collectives  15.3 us (19%)
  Pallas kernels  12.7 us (16%)
  local copies, waits for them, and re-layouts  7.62 us (9%)
    all_to_all x1, blocking collectives, local(): back = lax.all_to_all(back, 'lon', 0, 0, tiled=True)  15.3 us
    all_to_all x1, starting transfers between devices, local(): circle = lax.all_to_all(slots, 'lon', 0, 0, tiled=True)  8.8 us
    ppermute x2, waiting for transfers between devices, towards(): lax.ppermute(lax.dynamic_slice_in_dim(u, start, 2, axis=0), ('lat', 'lon'...  8.34 us
    ppermute x2, starting transfers between devices, towards(): lax.ppermute(lax.dynamic_slice_in_dim(u, start, 2, axis=0), ('lat', 'lon'...  7.57 us
    ppermute x1, starting transfers between devices, local(): lax.ppermute(jnp.concatenate([upper, eu, lower], axis=0), 'lon', [(j, (j...  6.06 us
    pallas_call x1, Pallas kernels, attention(): pl.pallas_call(attention_kernel, out_shape=jax.ShapeDtypeStruct((blocks,...  5.6 us
    ppermute x1, waiting for transfers between devices, local(): lax.ppermute(mixed_field[:, :MARGIN], 'lon', [(j, (j + 1) % columns) for...  4.9 us
    all_to_all x1, waiting for transfers between devices, local(): circle = lax.all_to_all(slots, 'lon', 0, 0, tiled=True)  4.59 us
  transfers between devices with their start and end apart: 5, of which 4 were waited for; matrix products, arithmetic and copies ran while one was open for 5% of the time, Pallas kernels for 3%

profile of v2, /device:TPU:1, one launch (start us, length us, event | category | flops | bytes accessed | tf_op | source)
XLA Modules:
  0.0 80.4 jit_solution(8272329117464777160)
XLA Ops:
  0.6 0.0 copy-start.2
  0.6 0.0 copy-start.3
  0.7 1.2 %dynamic-slice_bitcast_fusion = (bf16[2,64,1024]{2,1,0:T(8,128)(2,1)S(1)}, bf16[2,64,1024]{2,1,0:T(8,128)(2,1)S(1)}) fusion(bf16[1,4,64,1024]{3,2,1,0:T(8,128)(2,1)} %param.6, s32[]{:T(128)S(6)} %select_n.34, s32[]{:T(128)S(6)} %select_n.33), kind=kLoop, calls=%fused_computation | loop fusion | bytes 1048584 | tf_op jit(solution)/shard_map/dynamic_slice | solution.py:297
  1.8 4.0 %collective-permute-start.1 = (bf16[2,64,1024]{2,1,0:T(8,128)(2,1)S(1)}, bf16[2,64,1024]{2,1,0:T(8,128)(2,1)S(1)}, u32[]{:S(2)}, u32[]{:S(2)}) collective-permute-start(bf16[2,64,1024]{2,1,0:T(8,128)(2,1)S(1)} %get-tuple-element.16), channel_id=1, source_target_pairs={{0,16},{1,17},{2,18},{3,19},{4,20},{5,21},{6,22},{7,23},{8,0},{9,1... | collective-permute-start | bytes 786440 | tf_op jit(solution)/shard_map/ppermute | solution.py:296
  5.9 3.5 %collective-permute-start = (bf16[2,64,1024]{2,1,0:T(8,128)(2,1)S(1)}, bf16[2,64,1024]{2,1,0:T(8,128)(2,1)S(1)}, u32[]{:S(2)}, u32[]{:S(2)}) collective-permute-start(bf16[2,64,1024]{2,1,0:T(8,128)(2,1)S(1)} %get-tuple-element.17), channel_id=1, source_target_pairs={{0,8},{1,9},{2,10},{3,11},{4,12},{5,13},{6,14},{7,15},{8,24},{9,25... | collective-permute-start | bytes 786440 | tf_op jit(solution)/shard_map/ppermute | solution.py:296
  9.4 0.8 copy.8.one_ref
  10.2 0.8 copy.9.two_ref
  10.9 0.9 %slice.18 = bf16[4,4,1024]{2,1,0:T(4,128)(2,1)S(1)} slice(bf16[4,64,1024]{2,1,0:T(8,128)(2,1)} %bitcast.12), slice={[0:4], [0:4], [0:1024]} | slice | bytes 65536 | tf_op jit(solution)/shard_map/slice | solution.py:304
  11.8 6.1 %collective-permute-done.1.b_ref = bf16[2,64,1024]{2,1,0:T(8,128)(2,1)S(1)} collective-permute-done((bf16[2,64,1024]{2,1,0:T(8,128)(2,1)S(1)}, bf16[2,64,1024]{2,1,0:T(8,128)(2,1)S(1)}, u32[]{:S(2)}, u32[]{:S(2)}) %collective-permute-start.1) | collective-permute-done | bytes 262176 | tf_op jit(solution)/shard_map/ppermute | solution.py:296
  17.9 2.3 %collective-permute-done.a_ref = bf16[2,64,1024]{2,1,0:T(8,128)(2,1)S(1)} collective-permute-done((bf16[2,64,1024]{2,1,0:T(8,128)(2,1)S(1)}, bf16[2,64,1024]{2,1,0:T(8,128)(2,1)S(1)}, u32[]{:S(2)}, u32[]{:S(2)}) %collective-permute-start) | collective-permute-done | bytes 262176 | tf_op jit(solution)/shard_map/ppermute | solution.py:296
  20.2 0.1 pad_maximum_fusion
  20.3 6.1 %collective-permute-start.2 = (bf16[8,4,1024]{2,1,0:T(4,128)(2,1)S(1)}, bf16[8,4,1024]{2,1,0:T(4,128)(2,1)S(1)}, u32[]{:S(2)}, u32[]{:S(2)}) collective-permute-start(bf16[8,4,1024]{2,1,0:T(4,128)(2,1)S(1)} %pad_maximum_fusion), channel_id=1, source_target_pairs={{0,15},{1,0},{2,1},{3,2},{4,3},{5,4},{6,5},{7,6},{8,7},{9,8},{10,9... | collective-permute-start | bytes 196616 | tf_op jit(solution)/shard_map/ppermute | solution.py:308
  26.4 0.1 add_convert_fusion.flag_ref
  26.4 0.0 copy-start
  26.4 1.0 %copy-done = bf16[1,4,64,1024]{3,2,1,0:T(8,128)(2,1)S(1)} copy-done((bf16[1,4,64,1024]{3,2,1,0:T(8,128)(2,1)S(1)}, bf16[1,4,64,1024]{3,2,1,0:T(8,128)(2,1)}, u32[]{:S(2)}) %copy-start) | copy-done | bytes 524312
  27.5 2.6 %inner.1 = (bf16[4,64,1024]{2,1,0:T(8,128)(2,1)S(1)}, bf16[8,8,1024]{2,1,0:T(8,128)(2,1)S(1)}) custom-call(f32[8]{0:T(128)S(1)} %sine_abs_fusion.c_ref, s32[3]{0:T(128)S(1)} %add_convert_fusion.flag_ref, bf16[4,64,1024]{2,1,0:T(8,128)(2,1)S(1)} %bitcast.13, bf16[2,64,1024]{2,1,0:T(8,128)(2,1)S(1)} %collective-permute-done.a_ref, ...), custom_call_target="tpu_custom_call" | custom-call | flops 10485760 | bytes 8388608 | tf_op jit(solution)/shard_map/inner/pallas_call | solution.py:112
  30.1 0.0 collective-permute-done.2.edge_ref
  30.1 0.0 copy-done.2
  30.1 0.0 copy-done.3
  30.1 0.0 copy-start.1
  30.2 1.6 %copy-done.1 = bf16[1024,1024]{1,0:T(8,128)(2,1)S(1)} copy-done((bf16[1024,1024]{1,0:T(8,128)(2,1)S(1)}, bf16[1024,1024]{1,0:T(8,128)(2,1)}, u32[]{:S(2)}) %copy-start.1) | copy-done | bytes 2097176
  31.7 3.1 %project.1 = (bf16[4,64,1024]{2,1,0:T(8,128)(2,1)}, bf16[16,64,384]{2,1,0:T(8,128)(2,1)}) custom-call(f32[8]{0:T(128)S(1)} %sine_abs_fusion.c_ref, bf16[8,8,1024]{2,1,0:T(8,128)(2,1)S(1)} %get-tuple-element.8.side_ref, bf16[8,4,1024]{2,1,0:T(4,128)(2,1)S(1)} %collective-permute-done.2.edge_ref, bf16[4,64,1024]{2,1,0:T(8,128)(2,1)S(1)} %get-tuple-element.9.inner_ref, ...), custom_call_target="tpu_custom_call" | custom-call | flops 805306368 | bytes 6291456 | tf_op jit(solution)/shard_map/project/pallas_call | solution.py:203
  34.8 8.8 %all-to-all-start = ((bf16[16,64,384]{2,1,0:T(8,128)(2,1)}), bf16[16,64,384]{2,1,0:T(8,128)(2,1)S(1)}, u32[]{:S(2)}, u32[]{:S(2)}) async-start(bf16[16,64,384]{2,1,0:T(8,128)(2,1)} %get-tuple-element.10), calls=%async_computation | async-start | bytes 1572864 | tf_op jit(solution)/shard_map/all_to_all | solution.py:326
  43.6 0.8 %slice.15 = bf16[4,2,1024]{2,1,0:T(2,128)(2,1)S(1)} slice(bf16[4,64,1024]{2,1,0:T(8,128)(2,1)} %get-tuple-element.11), slice={[0:4], [0:2], [0:1024]} | slice | bytes 32768 | tf_op jit(solution)/shard_map/slice | solution.py:328
  44.5 3.5 %collective-permute-start.3 = (bf16[4,2,1024]{2,1,0:T(2,128)(2,1)S(1)}, bf16[4,2,1024]{2,1,0:T(2,128)(2,1)S(1)}, u32[]{:S(2)}, u32[]{:S(2)}) collective-permute-start(bf16[4,2,1024]{2,1,0:T(2,128)(2,1)S(1)} %slice.15), channel_id=1, source_target_pairs={{0,1},{1,2},{2,3},{3,4},{4,5},{5,6},{6,7},{7,8},{8,9},{9,10},{10,1... | collective-permute-start | bytes 49160 | tf_op jit(solution)/shard_map/ppermute | solution.py:327
  48.0 4.9 %collective-permute-done.3 = bf16[4,2,1024]{2,1,0:T(2,128)(2,1)S(1)} collective-permute-done((bf16[4,2,1024]{2,1,0:T(2,128)(2,1)S(1)}, bf16[4,2,1024]{2,1,0:T(2,128)(2,1)S(1)}, u32[]{:S(2)}, u32[]{:S(2)}) %collective-permute-start.3) | collective-permute-done | bytes 16416 | tf_op jit(solution)/shard_map/ppermute | solution.py:327
  52.9 0.6 constant_dynamic-update-slice_fusion
  53.5 4.6 %all-to-all-done = bf16[16,64,384]{2,1,0:T(8,128)(2,1)S(1)} async-done(((bf16[16,64,384]{2,1,0:T(8,128)(2,1)}), bf16[16,64,384]{2,1,0:T(8,128)(2,1)S(1)}, u32[]{:S(2)}, u32[]{:S(2)}) %all-to-all-start) | async-done | bytes 786464 | tf_op jit(solution)/shard_map/all_to_all | solution.py:326
  58.1 5.6 %attention.1 = bf16[16,64,256]{2,1,0:T(8,128)(2,1)S(1)} custom-call(bf16[1024,384]{1,0:T(8,128)(2,1)S(1)} %bitcast.14), custom_call_target="tpu_custom_call" | custom-call | flops 1073741824 | bytes 1310720 | tf_op jit(solution)/shard_map/attention/pallas_call | solution.py:253
  63.7 15.3 %all_to_all.10.x_ref = bf16[16,64,256]{2,1,0:T(8,128)(2,1)S(1)} all-to-all(bf16[16,64,256]{2,1,0:T(8,128)(2,1)S(1)} %attention.1), channel_id=1, replica_groups=mesh['lat'=32,'lon'=16] {'lon'}, dimensions={0} | all-to-all | bytes 1048576 | tf_op jit(solution)/shard_map/all_to_all | solution.py:333
  79.1 1.4 %gather_heads.1 = bf16[4,64,1024]{2,1,0:T(8,128)(2,1)} custom-call(bf16[16,64,256]{2,1,0:T(8,128)(2,1)S(1)} %all_to_all.10.x_ref), custom_call_target="tpu_custom_call" | custom-call | tf_op jit(solution)/shard_map/gather_heads/pallas_call | solution.py:274
  (3 shorter events, 0.1 us)
Async XLA Ops:
  0.6 29.5 %copy-start.2 = (bf16[1024,512]{1,0:T(8,128)(2,1)S(1)}, bf16[1024,512]{1,0:T(8,128)(2,1)}, u32[]{:S(2)}) copy-start(bf16[1024,512]{1,0:T(8,128)(2,1)} %wkv.1) | copy-start | bytes 3145732
  0.6 29.5 %copy-start.3 = (f32[1024]{0:T(1024)S(1)}, f32[1024]{0:T(1024)}, u32[]{:S(2)}) copy-start(f32[1024]{0:T(1024)} %param.9) | copy-start | bytes 12292
  1.8 16.1 %collective-permute-start.1 = (bf16[2,64,1024]{2,1,0:T(8,128)(2,1)S(1)}, bf16[2,64,1024]{2,1,0:T(8,128)(2,1)S(1)}, u32[]{:S(2)}, u32[]{:S(2)}) collective-permute-start(bf16[2,64,1024]{2,1,0:T(8,128)(2,1)S(1)} %get-tuple-element.16), channel_id=1, source_target_pairs={{0,16},{1,17},{2,18},{3,19},{4,20},{5,21},{6,22},{7,23},{8,0},{9,1... | collective-permute-start | bytes 786440 | tf_op jit(solution)/shard_map/ppermute | solution.py:296
  5.9 14.3 %collective-permute-start = (bf16[2,64,1024]{2,1,0:T(8,128)(2,1)S(1)}, bf16[2,64,1024]{2,1,0:T(8,128)(2,1)S(1)}, u32[]{:S(2)}, u32[]{:S(2)}) collective-permute-start(bf16[2,64,1024]{2,1,0:T(8,128)(2,1)S(1)} %get-tuple-element.17), channel_id=1, source_target_pairs={{0,8},{1,9},{2,10},{3,11},{4,12},{5,13},{6,14},{7,15},{8,24},{9,25... | collective-permute-start | bytes 786440 | tf_op jit(solution)/shard_map/ppermute | solution.py:296
  20.3 9.8 %collective-permute-start.2 = (bf16[8,4,1024]{2,1,0:T(4,128)(2,1)S(1)}, bf16[8,4,1024]{2,1,0:T(4,128)(2,1)S(1)}, u32[]{:S(2)}, u32[]{:S(2)}) collective-permute-start(bf16[8,4,1024]{2,1,0:T(4,128)(2,1)S(1)} %pad_maximum_fusion), channel_id=1, source_target_pairs={{0,15},{1,0},{2,1},{3,2},{4,3},{5,4},{6,5},{7,6},{8,7},{9,8},{10,9... | collective-permute-start | bytes 196616 | tf_op jit(solution)/shard_map/ppermute | solution.py:308
  26.4 1.0 %copy-start = (bf16[1,4,64,1024]{3,2,1,0:T(8,128)(2,1)S(1)}, bf16[1,4,64,1024]{3,2,1,0:T(8,128)(2,1)}, u32[]{:S(2)}) copy-start(bf16[1,4,64,1024]{3,2,1,0:T(8,128)(2,1)} %param.6) | copy-start | bytes 1572868
  30.1 1.6 %copy-start.1 = (bf16[1024,1024]{1,0:T(8,128)(2,1)S(1)}, bf16[1024,1024]{1,0:T(8,128)(2,1)}, u32[]{:S(2)}) copy-start(bf16[1024,1024]{1,0:T(8,128)(2,1)} %wq.1) | copy-start | bytes 6291460
  34.8 23.3 %all-to-all-start = ((bf16[16,64,384]{2,1,0:T(8,128)(2,1)}), bf16[16,64,384]{2,1,0:T(8,128)(2,1)S(1)}, u32[]{:S(2)}, u32[]{:S(2)}) async-start(bf16[16,64,384]{2,1,0:T(8,128)(2,1)} %get-tuple-element.10), calls=%async_computation | async-start | bytes 1572864 | tf_op jit(solution)/shard_map/all_to_all | solution.py:326
  44.5 8.4 %collective-permute-start.3 = (bf16[4,2,1024]{2,1,0:T(2,128)(2,1)S(1)}, bf16[4,2,1024]{2,1,0:T(2,128)(2,1)S(1)}, u32[]{:S(2)}, u32[]{:S(2)}) collective-permute-start(bf16[4,2,1024]{2,1,0:T(2,128)(2,1)S(1)} %slice.15), channel_id=1, source_target_pairs={{0,1},{1,2},{2,3},{3,4},{4,5},{5,6},{6,7},{7,8},{8,9},{9,10},{10,1... | collective-permute-start | bytes 49160 | tf_op jit(solution)/shard_map/ppermute | solution.py:327

commit v3 on v2

--- a/solution.py
+++ b/solution.py
@@ -79,7 +79,7 @@
 
         def row(r):
             if 2 <= r < rows + 2:
-                main = u_ref[r - 2, :, lanes].astype(jnp.float32)
+                main = u_ref[r - 2, :, lanes]
             elif r < 2:
                 i = jnp.where(north == 1, 1 - r, r)
                 main = jnp.where(
@@ -133,12 +133,20 @@
     one_ref,
     two_ref,
     gain_ref,
-    wq,
     wkv,
+    wq0,
+    wq1,
+    wq2,
+    wq3,
+    mixed_hbm,
+    slots_hbm,
+    head_ref,
     mixed_ref,
     slots_ref,
     strip,
     normed,
+    sems,
+    slot_sems,
 ):
     rows, cols, channels = inner_ref.shape
     margin = edge_ref.shape[1]
@@ -165,6 +173,7 @@
 
     lax.fori_loop(0, channels // LANES, chunk, 0, unroll=2)
     place = lax.broadcasted_iota(jnp.int32, (8, channels), 0)
+    copies = []
     for r in range(rows):
         m = inner_ref[r].astype(jnp.float32)
         m = jnp.concatenate(
@@ -176,6 +185,9 @@
             axis=0,
         ).astype(jnp.bfloat16)
         mixed_ref[r] = m
+        head_ref[r] = m[: 2 * 8]
+        copies.append(pltpu.make_async_copy(mixed_ref.at[r], mixed_hbm.at[r], sems.at[r]))
+        copies[r].start()
         m = m.astype(jnp.float32)
         mean_square = jnp.sum(m * m, axis=1, keepdims=True) * (1.0 / channels)
         normed[r * cols : (r + 1) * cols, :] = (
@@ -184,8 +196,8 @@
     x = normed[...]
     kv = jnp.dot(x, wkv[...], preferred_element_type=jnp.float32).astype(jnp.bfloat16)
     kw = KV_HEADS * HEAD_DIM
-    for g in range(KV_HEADS):
-        q = jnp.dot(x, wq[:, g * QW : (g + 1) * QW], preferred_element_type=jnp.float32)
+    for g, wq in enumerate((wq0, wq1, wq2, wq3)):
+        q = jnp.dot(x, wq[...], preferred_element_type=jnp.float32)
         q = (q * (math.log2(math.e) / math.sqrt(HEAD_DIM))).astype(jnp.bfloat16)
         at = g * HEAD_DIM
         pair = jnp.concatenate(
@@ -195,22 +207,35 @@
             here = slice(r * cols, (r + 1) * cols)
             slots_ref[r * KV_HEADS + g, :, :QW] = q[here]
             slots_ref[r * KV_HEADS + g, :, QW:] = pair[here]
+            at = r * KV_HEADS + g
+            copies.append(
+                pltpu.make_async_copy(slots_ref.at[at], slots_hbm.at[at], slot_sems.at[at])
+            )
+            copies[-1].start()
+    for copy in copies:
+        copy.wait()
 
 
 def project(c, side, edge, mixed, one, two, gain, wq, wkv):
     rows, cols, channels = mixed.shape
     vmem, smem = pl.BlockSpec(memory_space=pltpu.VMEM), pl.BlockSpec(memory_space=pltpu.SMEM)
+    hbm = pl.BlockSpec(memory_space=pltpu.HBM)
     return pl.pallas_call(
         project_kernel,
         out_shape=(
             jax.ShapeDtypeStruct((rows, cols, channels), jnp.bfloat16),
             jax.ShapeDtypeStruct((rows * KV_HEADS, cols, SLOT), jnp.bfloat16),
-        ),
-        in_specs=[smem] + [vmem] * 8,
-        out_specs=(vmem, vmem),
+            jax.ShapeDtypeStruct((rows, 16, channels), jnp.bfloat16),
+        ),
+        in_specs=[smem] + [vmem] * (7 + KV_HEADS),
+        out_specs=(hbm, hbm, vmem),
         scratch_shapes=[
+            pltpu.VMEM((rows, cols, channels), jnp.bfloat16),
+            pltpu.VMEM((rows * KV_HEADS, cols, SLOT), jnp.bfloat16),
             pltpu.VMEM((rows, 16, channels), jnp.float32),
             pltpu.VMEM((rows * cols, channels), jnp.bfloat16),
+            pltpu.SemaphoreType.DMA((rows,)),
+            pltpu.SemaphoreType.DMA((rows * KV_HEADS,)),
         ],
         compiler_params=pltpu.CompilerParams(vmem_limit_bytes=VMEM_LIMIT),
         cost_estimate=pl.CostEstimate(
@@ -219,28 +244,32 @@
             transcendentals=0,
         ),
         name="project",
-    )(c, side, edge, mixed, one, two, gain, wq, wkv)
+    )(c, side, edge, mixed, one, two, gain, wkv, *wq)
 
 
 def attention_kernel(x_ref, o_ref):
     blocks, cols, _ = o_ref.shape
     n = blocks * cols
-    k = x_ref[:, QW : QW + HEAD_DIM]
+    kt = x_ref[:, QW : QW + HEAD_DIM].T
     ones = jnp.ones((n, HEAD_DIM), jnp.bfloat16)
     v = jnp.concatenate([x_ref[:, QW + HEAD_DIM :], ones], axis=1)
     step = n // 2
-    for i in range(0, n, step):
-        outs = []
-        for h in range(GROUPS):
-            q = x_ref[i : i + step, h * HEAD_DIM : (h + 1) * HEAD_DIM]
-            s = lax.dot_general(
-                q, k, (((1,), (1,)), ((), ())), preferred_element_type=jnp.float32
-            )
-            p = jnp.exp2(s - jnp.max(s, axis=1, keepdims=True)).astype(jnp.bfloat16)
-            o = jnp.dot(p, v, preferred_element_type=jnp.float32)
-            outs.append(o[:, :HEAD_DIM] / o[:, HEAD_DIM:])
-        o = jnp.concatenate(outs, axis=1).astype(jnp.bfloat16)
-        o_ref[i // cols : (i + step) // cols] = o.reshape(step // cols, cols, QW)
+    work = [(i, h) for i in range(0, n, step) for h in range(GROUPS)]
+
+    def scores(i, h):
+        q = x_ref[i : i + step, h * HEAD_DIM : (h + 1) * HEAD_DIM]
+        return jnp.dot(q, kt, preferred_element_type=jnp.float32)
+
+    outs, ready = [], scores(*work[0])
+    for w, (i, h) in enumerate(work):
+        s, ready = ready, scores(*work[w + 1]) if w + 1 < len(work) else None
+        p = jnp.exp2(s - jnp.max(s, axis=1, keepdims=True)).astype(jnp.bfloat16)
+        o = jnp.dot(p, v, preferred_element_type=jnp.float32)
+        outs.append(o[:, :HEAD_DIM] / o[:, HEAD_DIM:])
+        if h == GROUPS - 1:
+            o = jnp.concatenate(outs, axis=1).astype(jnp.bfloat16)
+            o_ref[i // cols : (i + step) // cols] = o.reshape(step // cols, cols, QW)
+            outs = []
     tile = 16
     heads = [o_ref[b, :tile, :] for b in range(blocks)]
     moved = lax.broadcasted_iota(jnp.int32, (tile, QW), 0) < MARGIN
@@ -265,21 +294,44 @@
     )(x)
 
 
-def gather_heads_kernel(x_ref, o_ref):
-    for g in range(KV_HEADS):
-        o_ref[0, :, g * QW : (g + 1) * QW] = x_ref[g]
-
-
-def gather_heads(x, rows, cols, channels):
+def gather_heads_kernel(x_ref, head_ref, displaced_ref, _, o_hbm, mixed_hbm, staged, tile, sems):
+    rows, margin, channels = displaced_ref.shape
+    copies = []
+    moved = lax.broadcasted_iota(jnp.int32, (16, channels), 0) < margin
+    pad = jnp.zeros((16 - margin, channels), jnp.float32)
+    for r in range(rows):
+        new = jnp.concatenate([displaced_ref[r].astype(jnp.float32), pad], axis=0)
+        tile[r] = jnp.where(moved, new, head_ref[r].astype(jnp.float32)).astype(jnp.bfloat16)
+        copies.append(
+            pltpu.make_async_copy(tile.at[r], mixed_hbm.at[r, pl.ds(0, 16)], sems.at[rows + r])
+        )
+        copies[-1].start()
+        for g in range(KV_HEADS):
+            staged[r, :, g * QW : (g + 1) * QW] = x_ref[r * KV_HEADS + g]
+        copies.append(pltpu.make_async_copy(staged.at[r], o_hbm.at[r], sems.at[r]))
+        copies[-1].start()
+    for copy in copies:
+        copy.wait()
+
+
+def gather_heads(x, head, displaced, mixed):
+    rows, cols, channels = mixed.shape
+    vmem, hbm = pl.BlockSpec(memory_space=pltpu.VMEM), pl.BlockSpec(memory_space=pltpu.HBM)
+    whole = jax.ShapeDtypeStruct((rows, cols, channels), jnp.bfloat16)
     return pl.pallas_call(
         gather_heads_kernel,
-        grid=(rows,),
-        out_shape=jax.ShapeDtypeStruct((rows, cols, channels), jnp.bfloat16),
-        in_specs=[pl.BlockSpec((KV_HEADS, cols, QW), lambda r: (r, 0, 0))],
-        out_specs=pl.BlockSpec((1, cols, channels), lambda r: (r, 0, 0)),
+        out_shape=(whole, whole),
+        in_specs=[vmem, vmem, vmem, hbm],
+        out_specs=(hbm, hbm),
+        input_output_aliases={3: 1},
+        scratch_shapes=[
+            pltpu.VMEM((rows, cols, channels), jnp.bfloat16),
+            pltpu.VMEM((rows, 16, channels), jnp.bfloat16),
+            pltpu.SemaphoreType.DMA((2 * rows,)),
+        ],
         compiler_params=pltpu.CompilerParams(vmem_limit_bytes=VMEM_LIMIT),
         name="gather_heads",
-    )(x)
+    )(x, head, displaced, mixed)
 
 
 def local(grid_state, stencil_one, stencil_two, norm_gain, query_weight, key_value_weight):
@@ -291,15 +343,13 @@
     west = lon < columns // 2
     first, last = lat == 0, lat == bands - 1
 
-    def towards(west_north):
+    def rim(west_north):
         start = jnp.where(west == west_north, 0, rows - 2)
-        return lax.ppermute(
-            lax.dynamic_slice_in_dim(u, start, 2, axis=0),
-            ("lat", "lon"),
-            meridian_pairs(bands, columns, west_north),
-        )
-
-    a, b = towards(True), towards(False)
+        return lax.dynamic_slice_in_dim(u, start, 2, axis=0)
+
+    rim_a, rim_b, u = lax.optimization_barrier((rim(True), rim(False), u))
+    a = lax.ppermute(rim_a, ("lat", "lon"), meridian_pairs(bands, columns, True))
+    b = lax.ppermute(rim_b, ("lat", "lon"), meridian_pairs(bands, columns, False))
 
     ea, eb, eu = a[:, : 2 * MARGIN], b[:, : 2 * MARGIN], u[:, : 2 * MARGIN]
     lower, upper = jnp.where(west, ea, eb), jnp.where(west, eb, ea)
@@ -311,8 +361,8 @@
         [(j, (j - 1) % columns) for j in range(columns)],
     )
     flags = jnp.stack([west, first, last]).astype(jnp.int32)
-    mixed_inner, side = inner(c, flags, u, a, b, stencil_one, stencil_two)
-    mixed_field, slots = project(
+    mixed_inner, side = inner(c, flags, u.astype(jnp.float32), a, b, stencil_one, stencil_two)
+    mixed_field, slots, head_tile = project(
         c,
         side,
         edge,
@@ -320,18 +370,17 @@
         stencil_one,
         stencil_two,
         norm_gain[None],
-        query_weight,
+        [query_weight[:, g * QW : (g + 1) * QW] for g in range(KV_HEADS)],
         key_value_weight,
     )
     circle = lax.all_to_all(slots, "lon", 0, 0, tiled=True)
     displaced = lax.ppermute(
-        mixed_field[:, :MARGIN], "lon", [(j, (j + 1) % columns) for j in range(columns)]
+        head_tile[:, :MARGIN], "lon", [(j, (j + 1) % columns) for j in range(columns)]
     )
-    mixed_field = lax.dynamic_update_slice(mixed_field, displaced, (0, 0, 0))
-    circle, mixed_field = lax.optimization_barrier((circle, mixed_field))
+    circle, displaced = lax.optimization_barrier((circle, displaced))
     back = attention(circle.reshape(-1, SLOT), columns)
     back = lax.all_to_all(back, "lon", 0, 0, tiled=True)
-    attended = gather_heads(back, rows, cols, channels)
+    attended, mixed_field = gather_heads(back, head_tile, displaced, mixed_field)
     return mixed_field[None], attended[None]
 
 

time: 81.1 us -> 78.7 us (0.970)
  waiting for transfers between devices: 17.8 us -> 23.4 us
  starting transfers between devices: 26 us -> 21.4 us
  local copies, waits for them, and re-layouts: 7.62 us -> 3.75 us
  other arithmetic: 0.21 us -> 1.36 us
  Pallas kernels: 12.7 us -> 11.7 us
    ppermute x3, waiting for transfers between devices: 13.2 us -> 17.8 us  [the longest x1 7.02 us: local(): lax.ppermute(rim_b, ('lat', 'lon'), meridian_pairs(bands, columns, False))]
    unnamed x10, local copies, waits for them, and re-layouts: 4.15 us -> 0.05 us
    ppermute x1, starting transfers between devices: 6.06 us -> 3.46 us  [local(): lax.ppermute(jnp.concatenate([upper, eu, lower], axis=0), 'lon', [(j, (j...]
    all_to_all x1, starting transfers between devices: 8.8 us -> 6.88 us  [local(): circle = lax.all_to_all(slots, 'lon', 0, 0, tiled=True)]
    convert_element_type x0 -> x1, other arithmetic: none -> 1.15 us  [local(): u.astype(jnp.float32)]
    slice x1 -> x2, local copies, waits for them, and re-layouts: 0.85 us -> 1.78 us  [the longest x1 1.77 us: local(): query_weight[:, g * QW:(g + 1) * QW]]
  transfers between devices with their start and end apart: 5 -> 5, of which waited for: 4 -> 5; matrix products, arithmetic and copies ran while one was open for 5% -> 5% of each run, Pallas kernels for 3% -> 3%
where the time goes in v3:
time: 78.7 us; the launch traced here: 77.3 us
  waiting for transfers between devices  23.4 us (30%)
  starting transfers between devices  21.4 us (27%)
  blocking collectives  14.9 us (19%)
  Pallas kernels  11.7 us (15%)
  local copies, waits for them, and re-layouts  3.75 us (5%)
  other arithmetic  1.36 us (2%)
  between operations  0.81 us (1%)
    all_to_all x1, blocking collectives, local(): back = lax.all_to_all(back, 'lon', 0, 0, tiled=True)  14.9 us
    ppermute x1, waiting for transfers between devices, local(): lax.ppermute(rim_b, ('lat', 'lon'), meridian_pairs(bands, columns, False))  7.02 us
    all_to_all x1, starting transfers between devices, local(): circle = lax.all_to_all(slots, 'lon', 0, 0, tiled=True)  6.88 us
    ppermute x1, waiting for transfers between devices, local(): lax.ppermute(head_tile[:, :MARGIN], 'lon', [(j, (j + 1) % columns) for j...  5.73 us
    ppermute x1, starting transfers between devices, local(): lax.ppermute(rim_a, ('lat', 'lon'), meridian_pairs(bands, columns, True))  5.65 us
    all_to_all x1, waiting for transfers between devices, local(): circle = lax.all_to_all(slots, 'lon', 0, 0, tiled=True)  5.2 us
    pallas_call x1, Pallas kernels, attention(): pl.pallas_call(attention_kernel, out_shape=jax.ShapeDtypeStruct((blocks,...  5.13 us
    ppermute x1, waiting for transfers between devices, local(): lax.ppermute(rim_a, ('lat', 'lon'), meridian_pairs(bands, columns, True))  5.05 us
  transfers between devices with their start and end apart: 5, of which 5 were waited for; matrix products, arithmetic and copies ran while one was open for 5% of the time, Pallas kernels for 3%

profile of v3, /device:TPU:1, one launch (start us, length us, event | category | flops | bytes accessed | tf_op | source)
XLA Modules:
  0.0 77.3 jit_solution(8618541207876305114)
XLA Ops:
  0.6 0.0 copy-start.2
  0.6 0.0 copy-start.3
  0.7 1.1 %dynamic-slice_bitcast_fusion = (bf16[2,64,1024]{2,1,0:T(8,128)(2,1)S(1)}, bf16[2,64,1024]{2,1,0:T(8,128)(2,1)S(1)}) fusion(bf16[1,4,64,1024]{3,2,1,0:T(8,128)(2,1)} %param.6, s32[]{:T(128)S(6)} %select_n.34, s32[]{:T(128)S(6)} %select_n.33), kind=kLoop, calls=%fused_computation | loop fusion | bytes 1048584 | tf_op jit(solution)/shard_map/dynamic_slice | solution.py:348
  1.7 5.7 %collective-permute-start = (bf16[2,64,1024]{2,1,0:T(8,128)(2,1)S(1)}, bf16[2,64,1024]{2,1,0:T(8,128)(2,1)S(1)}, u32[]{:S(2)}, u32[]{:S(2)}) collective-permute-start(bf16[2,64,1024]{2,1,0:T(8,128)(2,1)S(1)} %get-tuple-element.15), channel_id=1, source_target_pairs={{0,8},{1,9},{2,10},{3,11},{4,12},{5,13},{6,14},{7,15},{8,24},{9,25... | collective-permute-start | bytes 786440 | tf_op jit(solution)/shard_map/ppermute | solution.py:351
  7.4 1.9 %collective-permute-start.1 = (bf16[2,64,1024]{2,1,0:T(8,128)(2,1)S(1)}, bf16[2,64,1024]{2,1,0:T(8,128)(2,1)S(1)}, u32[]{:S(2)}, u32[]{:S(2)}) collective-permute-start(bf16[2,64,1024]{2,1,0:T(8,128)(2,1)S(1)} %get-tuple-element.16), channel_id=1, source_target_pairs={{0,16},{1,17},{2,18},{3,19},{4,20},{5,21},{6,22},{7,23},{8,0},{9,1... | collective-permute-start | bytes 786440 | tf_op jit(solution)/shard_map/ppermute | solution.py:352
  9.3 0.9 %slice.26 = bf16[4,4,1024]{2,1,0:T(4,128)(2,1)S(1)} slice(bf16[4,64,1024]{2,1,0:T(8,128)(2,1)} %bitcast.14), slice={[0:4], [0:4], [0:1024]} | slice | bytes 65536 | tf_op jit(solution)/shard_map/slice | solution.py:354
  10.2 1.1 %convert_element_type.11.u_ref = f32[4,64,1024]{2,1,0:T(8,128)S(1)} convert(bf16[4,64,1024]{2,1,0:T(8,128)(2,1)} %bitcast.15) | non-fusion elementwise | flops 262144 | bytes 1572864 | tf_op jit(solution)/shard_map/convert_element_type | solution.py:364
  11.4 0.0 copy-done.2
  11.4 0.0 copy-done.3
  11.5 0.0 copy-start
  11.5 0.0 copy-start.1
  11.5 1.8 %fusion = (bf16[1024,256]{1,0:T(8,128)(2,1)S(1)}, bf16[1024,256]{1,0:T(8,128)(2,1)S(1)}, bf16[1024,256]{1,0:T(8,128)(2,1)S(1)}, bf16[1024,256]{1,0:T(8,128)(2,1)S(1)}) fusion(bf16[1024,1024]{1,0:T(8,128)(2,1)} %param.10), kind=kLoop, calls=%fused_computation.9 | loop fusion | bytes 4194304 | tf_op jit(solution)/shard_map/slice | solution.py:373
  13.2 5.0 %collective-permute-done.a_ref = bf16[2,64,1024]{2,1,0:T(8,128)(2,1)S(1)} collective-permute-done((bf16[2,64,1024]{2,1,0:T(8,128)(2,1)S(1)}, bf16[2,64,1024]{2,1,0:T(8,128)(2,1)S(1)}, u32[]{:S(2)}, u32[]{:S(2)}) %collective-permute-start) | collective-permute-done | bytes 262176 | tf_op jit(solution)/shard_map/ppermute | solution.py:351
  18.3 7.0 %collective-permute-done.1.b_ref = bf16[2,64,1024]{2,1,0:T(8,128)(2,1)S(1)} collective-permute-done((bf16[2,64,1024]{2,1,0:T(8,128)(2,1)S(1)}, bf16[2,64,1024]{2,1,0:T(8,128)(2,1)S(1)}, u32[]{:S(2)}, u32[]{:S(2)}) %collective-permute-start.1) | collective-permute-done | bytes 262176 | tf_op jit(solution)/shard_map/ppermute | solution.py:352
  25.4 0.1 pad_maximum_fusion
  25.4 3.5 %collective-permute-start.2 = (bf16[8,4,1024]{2,1,0:T(4,128)(2,1)S(1)}, bf16[8,4,1024]{2,1,0:T(4,128)(2,1)S(1)}, u32[]{:S(2)}, u32[]{:S(2)}) collective-permute-start(bf16[8,4,1024]{2,1,0:T(4,128)(2,1)S(1)} %pad_maximum_fusion), channel_id=1, source_target_pairs={{0,15},{1,0},{2,1},{3,2},{4,3},{5,4},{6,5},{7,6},{8,7},{9,8},{10,9... | collective-permute-start | bytes 196616 | tf_op jit(solution)/shard_map/ppermute | solution.py:358
  28.9 0.1 add_convert_fusion.flag_ref
  29.0 2.6 %inner.1 = (bf16[4,64,1024]{2,1,0:T(8,128)(2,1)S(1)}, bf16[8,8,1024]{2,1,0:T(8,128)(2,1)S(1)}) custom-call(f32[8]{0:T(128)S(1)} %sine_abs_fusion.c_ref, s32[3]{0:T(128)S(1)} %add_convert_fusion.flag_ref, f32[4,64,1024]{2,1,0:T(8,128)S(1)} %convert_element_type.11.u_ref, bf16[2,64,1024]{2,1,0:T(8,128)(2,1)S(1)} %collective-permute-done.a_ref, ...), custom_call_target="tpu_custom_call" | custom-call | flops 10485760 | bytes 8388608 | tf_op jit(solution)/shard_map/inner/pallas_call | solution.py:112
  31.6 0.4 collective-permute-done.2.edge_ref
  31.9 0.0 copy-done
  31.9 0.0 copy-done.1
  31.9 3.1 %project.1 = (bf16[4,64,1024]{2,1,0:T(8,128)(2,1)}, bf16[16,64,384]{2,1,0:T(8,128)(2,1)}, bf16[4,16,1024]{2,1,0:T(8,128)(2,1)S(1)}) custom-call(f32[8]{0:T(128)S(1)} %sine_abs_fusion.c_ref, bf16[8,8,1024]{2,1,0:T(8,128)(2,1)S(1)} %get-tuple-element.17.side_ref, bf16[8,4,1024]{2,1,0:T(4,128)(2,1)S(1)} %collective-permute-done.2.edge_ref, ...), custom_call_target="tpu_custom_call" | custom-call | flops 805306368 | bytes 6291456 | tf_op jit(solution)/shard_map/project/pallas_call | solution.py:223
  35.1 6.9 %all-to-all-start = ((bf16[16,64,384]{2,1,0:T(8,128)(2,1)}), bf16[16,64,384]{2,1,0:T(8,128)(2,1)S(1)}, u32[]{:S(2)}, u32[]{:S(2)}) async-start(bf16[16,64,384]{2,1,0:T(8,128)(2,1)} %get-tuple-element.19), calls=%async_computation | async-start | bytes 1572864 | tf_op jit(solution)/shard_map/all_to_all | solution.py:376
  42.0 3.5 %collective-permute-start.3 = (bf16[4,2,1024]{2,1,0:T(2,128)(2,1)S(1)}, bf16[4,2,1024]{2,1,0:T(2,128)(2,1)S(1)}, u32[]{:S(2)}, u32[]{:S(2)}) collective-permute-start(bf16[4,2,1024]{2,1,0:T(2,128)(2,1)S(1)} %slice.31), channel_id=1, source_target_pairs={{0,1},{1,2},{2,3},{3,4},{4,5},{5,6},{6,7},{7,8},{8,9},{9,10},{10,1... | collective-permute-start | bytes 49160 | tf_op jit(solution)/shard_map/ppermute | solution.py:377
  45.5 5.7 %collective-permute-done.3.displaced_ref = bf16[4,2,1024]{2,1,0:T(2,128)(2,1)S(1)} collective-permute-done((bf16[4,2,1024]{2,1,0:T(2,128)(2,1)S(1)}, bf16[4,2,1024]{2,1,0:T(2,128)(2,1)S(1)}, u32[]{:S(2)}, u32[]{:S(2)}) %collective-permute-start.3) | collective-permute-done | bytes 16416 | tf_op jit(solution)/shard_map/ppermute | solution.py:377
  51.2 5.2 %all-to-all-done = bf16[16,64,384]{2,1,0:T(8,128)(2,1)S(1)} async-done(((bf16[16,64,384]{2,1,0:T(8,128)(2,1)}), bf16[16,64,384]{2,1,0:T(8,128)(2,1)S(1)}, u32[]{:S(2)}, u32[]{:S(2)}) %all-to-all-start) | async-done | bytes 786464 | tf_op jit(solution)/shard_map/all_to_all | solution.py:376
  56.4 5.1 %attention.1 = bf16[16,64,256]{2,1,0:T(8,128)(2,1)S(1)} custom-call(bf16[1024,384]{1,0:T(8,128)(2,1)S(1)} %bitcast.12), custom_call_target="tpu_custom_call" | custom-call | flops 1073741824 | bytes 1310720 | tf_op jit(solution)/shard_map/attention/pallas_call | solution.py:282
  61.6 14.9 %all_to_all.10.x_ref = bf16[16,64,256]{2,1,0:T(8,128)(2,1)S(1)} all-to-all(bf16[16,64,256]{2,1,0:T(8,128)(2,1)S(1)} %attention.1), channel_id=1, replica_groups=mesh['lat'=32,'lon'=16] {'lon'}, dimensions={0} | all-to-all | bytes 1048576 | tf_op jit(solution)/shard_map/all_to_all | solution.py:382
  76.4 0.9 %gather_heads.1 = (bf16[4,64,1024]{2,1,0:T(8,128)(2,1)}, bf16[4,64,1024]{2,1,0:T(8,128)(2,1)}) custom-call(bf16[16,64,256]{2,1,0:T(8,128)(2,1)S(1)} %all_to_all.10.x_ref, bf16[4,16,1024]{2,1,0:T(8,128)(2,1)S(1)} %get-tuple-element.20.head_ref, bf16[4,2,1024]{2,1,0:T(2,128)(2,1)S(1)} %collective-permute-done.3.displaced_ref, ...), custom_call_target="tpu_custom_call", output_to_operand_aliasing={{1}: (3, {})} | custom-call | tf_op jit(solution)/shard_map/gather_heads/pallas_call | solution.py:321
  (6 shorter events, 0.1 us)
Async XLA Ops:
  0.6 10.8 %copy-start.2 = (f32[2,3,1024]{2,0,1:T(2,128)S(1)}, f32[2,3,1024]{2,0,1:T(2,128)}, u32[]{:S(2)}) copy-start(f32[2,3,1024]{2,0,1:T(2,128)} %param.7) | copy-start | bytes 73732
  0.6 10.8 %copy-start.3 = (f32[2,3,1024]{2,0,1:T(2,128)S(1)}, f32[2,3,1024]{2,0,1:T(2,128)}, u32[]{:S(2)}) copy-start(f32[2,3,1024]{2,0,1:T(2,128)} %param.8) | copy-start | bytes 73732
  1.7 16.6 %collective-permute-start = (bf16[2,64,1024]{2,1,0:T(8,128)(2,1)S(1)}, bf16[2,64,1024]{2,1,0:T(8,128)(2,1)S(1)}, u32[]{:S(2)}, u32[]{:S(2)}) collective-permute-start(bf16[2,64,1024]{2,1,0:T(8,128)(2,1)S(1)} %get-tuple-element.15), channel_id=1, source_target_pairs={{0,8},{1,9},{2,10},{3,11},{4,12},{5,13},{6,14},{7,15},{8,24},{9,25... | collective-permute-start | bytes 786440 | tf_op jit(solution)/shard_map/ppermute | solution.py:351
  7.4 17.9 %collective-permute-start.1 = (bf16[2,64,1024]{2,1,0:T(8,128)(2,1)S(1)}, bf16[2,64,1024]{2,1,0:T(8,128)(2,1)S(1)}, u32[]{:S(2)}, u32[]{:S(2)}) collective-permute-start(bf16[2,64,1024]{2,1,0:T(8,128)(2,1)S(1)} %get-tuple-element.16), channel_id=1, source_target_pairs={{0,16},{1,17},{2,18},{3,19},{4,20},{5,21},{6,22},{7,23},{8,0},{9,1... | collective-permute-start | bytes 786440 | tf_op jit(solution)/shard_map/ppermute | solution.py:352
  11.5 20.5 %copy-start = (bf16[1024,512]{1,0:T(8,128)(2,1)S(1)}, bf16[1024,512]{1,0:T(8,128)(2,1)}, u32[]{:S(2)}) copy-start(bf16[1024,512]{1,0:T(8,128)(2,1)} %wkv.1) | copy-start | bytes 3145732
  11.5 20.5 %copy-start.1 = (f32[1024]{0:T(1024)S(1)}, f32[1024]{0:T(1024)}, u32[]{:S(2)}) copy-start(f32[1024]{0:T(1024)} %param.9) | copy-start | bytes 12292
  25.4 6.5 %collective-permute-start.2 = (bf16[8,4,1024]{2,1,0:T(4,128)(2,1)S(1)}, bf16[8,4,1024]{2,1,0:T(4,128)(2,1)S(1)}, u32[]{:S(2)}, u32[]{:S(2)}) collective-permute-start(bf16[8,4,1024]{2,1,0:T(4,128)(2,1)S(1)} %pad_maximum_fusion), channel_id=1, source_target_pairs={{0,15},{1,0},{2,1},{3,2},{4,3},{5,4},{6,5},{7,6},{8,7},{9,8},{10,9... | collective-permute-start | bytes 196616 | tf_op jit(solution)/shard_map/ppermute | solution.py:358
  35.1 21.4 %all-to-all-start = ((bf16[16,64,384]{2,1,0:T(8,128)(2,1)}), bf16[16,64,384]{2,1,0:T(8,128)(2,1)S(1)}, u32[]{:S(2)}, u32[]{:S(2)}) async-start(bf16[16,64,384]{2,1,0:T(8,128)(2,1)} %get-tuple-element.19), calls=%async_computation | async-start | bytes 1572864 | tf_op jit(solution)/shard_map/all_to_all | solution.py:376
  42.0 9.3 %collective-permute-start.3 = (bf16[4,2,1024]{2,1,0:T(2,128)(2,1)S(1)}, bf16[4,2,1024]{2,1,0:T(2,128)(2,1)S(1)}, u32[]{:S(2)}, u32[]{:S(2)}) collective-permute-start(bf16[4,2,1024]{2,1,0:T(2,128)(2,1)S(1)} %slice.31), channel_id=1, source_target_pairs={{0,1},{1,2},{2,3},{3,4},{4,5},{5,6},{6,7},{7,8},{8,9},{9,10},{10,1... | collective-permute-start | bytes 49160 | tf_op jit(solution)/shard_map/ppermute | solution.py:377

commit v4 on v3

--- a/solution.py
+++ b/solution.py
@@ -14,6 +14,8 @@
 QW = GROUPS * HEAD_DIM
 SLOT = QW + 2 * HEAD_DIM
 MARGIN = 2
+STRIP_LANES = 512
+UNROLL = 1
 LANES = 128
 VMEM_LIMIT = 24 * 1024 * 1024
 
@@ -34,6 +36,35 @@
 def row_weights(first_row, row_count, nlat):
     positions = (jnp.arange(row_count, dtype=jnp.int32) + first_row).astype(jnp.float32)
     return jnp.abs(jnp.sin(jnp.pi * (positions + 0.5) / nlat))
+
+
+def rims_kernel(west_ref, u_hbm, a_ref, b_ref, sems):
+    count = a_ref.shape[0]
+    last = u_hbm.shape[0] - count
+    west = west_ref[0]
+    copies = [
+        pltpu.make_async_copy(u_hbm.at[pl.ds(last * (1 - west), count)], a_ref, sems.at[0]),
+        pltpu.make_async_copy(u_hbm.at[pl.ds(last * west, count)], b_ref, sems.at[1]),
+    ]
+    for copy in copies:
+        copy.start()
+    for copy in copies:
+        copy.wait()
+
+
+def rims(west, u):
+    rows, cols, channels = u.shape
+    rim = jax.ShapeDtypeStruct((2, cols, channels), jnp.bfloat16)
+    vmem = pl.BlockSpec(memory_space=pltpu.VMEM)
+    return pl.pallas_call(
+        rims_kernel,
+        out_shape=(rim, rim),
+        in_specs=[pl.BlockSpec(memory_space=pltpu.SMEM), pl.BlockSpec(memory_space=pltpu.HBM)],
+        out_specs=(vmem, vmem),
+        scratch_shapes=[pltpu.SemaphoreType.DMA((2,))],
+        compiler_params=pltpu.CompilerParams(vmem_limit_bytes=VMEM_LIMIT),
+        name="rims",
+    )(west, u)
 
 
 def add_stencil(before, here, after, raw, w_ref, lanes):
@@ -150,10 +181,10 @@
 ):
     rows, cols, channels = inner_ref.shape
     margin = edge_ref.shape[1]
-    pad = jnp.zeros((8 - margin, LANES), jnp.float32)
+    pad = jnp.zeros((8 - margin, STRIP_LANES), jnp.float32)
 
     def chunk(n, _):
-        lanes = pl.ds(pl.multiple_of(n * LANES, LANES), LANES)
+        lanes = pl.ds(pl.multiple_of(n * STRIP_LANES, STRIP_LANES), STRIP_LANES)
 
         def row(r):
             return jnp.concatenate(
@@ -171,45 +202,51 @@
         two_stencils(row, rows, c_ref, one_ref, two_ref, lanes, store)
         return 0
 
-    lax.fori_loop(0, channels // LANES, chunk, 0, unroll=2)
+    lax.fori_loop(0, channels // STRIP_LANES, chunk, 0, unroll=UNROLL)
     place = lax.broadcasted_iota(jnp.int32, (8, channels), 0)
     copies = []
-    for r in range(rows):
-        m = inner_ref[r].astype(jnp.float32)
-        m = jnp.concatenate(
-            [
-                jnp.where(place < MARGIN, strip[r, 8:], m[:8]),
-                m[8 : cols - 8],
-                jnp.where(place >= 8 - MARGIN, strip[r, :8], m[cols - 8 :]),
-            ],
-            axis=0,
-        ).astype(jnp.bfloat16)
-        mixed_ref[r] = m
-        head_ref[r] = m[: 2 * 8]
-        copies.append(pltpu.make_async_copy(mixed_ref.at[r], mixed_hbm.at[r], sems.at[r]))
-        copies[r].start()
-        m = m.astype(jnp.float32)
-        mean_square = jnp.sum(m * m, axis=1, keepdims=True) * (1.0 / channels)
-        normed[r * cols : (r + 1) * cols, :] = (
-            m * lax.rsqrt(mean_square + 1e-06) * gain_ref[...]
-        ).astype(jnp.bfloat16)
-    x = normed[...]
-    kv = jnp.dot(x, wkv[...], preferred_element_type=jnp.float32).astype(jnp.bfloat16)
     kw = KV_HEADS * HEAD_DIM
-    for g, wq in enumerate((wq0, wq1, wq2, wq3)):
-        q = jnp.dot(x, wq[...], preferred_element_type=jnp.float32)
-        q = (q * (math.log2(math.e) / math.sqrt(HEAD_DIM))).astype(jnp.bfloat16)
-        at = g * HEAD_DIM
-        pair = jnp.concatenate(
-            [kv[:, at : at + HEAD_DIM], kv[:, kw + at : kw + at + HEAD_DIM]], axis=1
-        )
-        for r in range(rows):
-            here = slice(r * cols, (r + 1) * cols)
-            slots_ref[r * KV_HEADS + g, :, :QW] = q[here]
-            slots_ref[r * KV_HEADS + g, :, QW:] = pair[here]
-            at = r * KV_HEADS + g
+    half = rows // 2
+    for start in range(0, rows, half):
+        for r in range(start, start + half):
+            m = inner_ref[r].astype(jnp.float32)
+            m = jnp.concatenate(
+                [
+                    jnp.where(place < MARGIN, strip[r, 8:], m[:8]),
+                    m[8 : cols - 8],
+                    jnp.where(place >= 8 - MARGIN, strip[r, :8], m[cols - 8 :]),
+                ],
+                axis=0,
+            ).astype(jnp.bfloat16)
+            mixed_ref[r] = m
+            head_ref[r] = m[: 2 * 8]
+            copies.append(pltpu.make_async_copy(mixed_ref.at[r], mixed_hbm.at[r], sems.at[r]))
+            copies[-1].start()
+            m = m.astype(jnp.float32)
+            mean_square = jnp.sum(m * m, axis=1, keepdims=True) * (1.0 / channels)
+            normed[r * cols : (r + 1) * cols, :] = (
+                m * lax.rsqrt(mean_square + 1e-06) * gain_ref[...]
+            ).astype(jnp.bfloat16)
+        x = normed[start * cols : (start + half) * cols, :]
+        kv = jnp.dot(x, wkv[...], preferred_element_type=jnp.float32).astype(jnp.bfloat16)
+        for g, wq in enumerate((wq0, wq1, wq2, wq3)):
+            q = jnp.dot(x, wq[...], preferred_element_type=jnp.float32)
+            q = (q * (math.log2(math.e) / math.sqrt(HEAD_DIM))).astype(jnp.bfloat16)
+            at = g * HEAD_DIM
+            pair = jnp.concatenate(
+                [kv[:, at : at + HEAD_DIM], kv[:, kw + at : kw + at + HEAD_DIM]], axis=1
+            )
+            for r in range(half):
+                here = slice(r * cols, (r + 1) * cols)
+                slots_ref[start + r, g, :, :QW] = q[here]
+                slots_ref[start + r, g, :, QW:] = pair[here]
+            part = pl.ds(start, half)
             copies.append(
-                pltpu.make_async_copy(slots_ref.at[at], slots_hbm.at[at], slot_sems.at[at])
+                pltpu.make_async_copy(
+                    slots_ref.at[part, g],
+                    slots_hbm.at[part, g],
+                    slot_sems.at[start // half * KV_HEADS + g],
+                )
             )
             copies[-1].start()
     for copy in copies:
@@ -224,18 +261,18 @@
         project_kernel,
         out_shape=(
             jax.ShapeDtypeStruct((rows, cols, channels), jnp.bfloat16),
-            jax.ShapeDtypeStruct((rows * KV_HEADS, cols, SLOT), jnp.bfloat16),
+            jax.ShapeDtypeStruct((rows, KV_HEADS, cols, SLOT), jnp.bfloat16),
             jax.ShapeDtypeStruct((rows, 16, channels), jnp.bfloat16),
         ),
         in_specs=[smem] + [vmem] * (7 + KV_HEADS),
         out_specs=(hbm, hbm, vmem),
         scratch_shapes=[
             pltpu.VMEM((rows, cols, channels), jnp.bfloat16),
-            pltpu.VMEM((rows * KV_HEADS, cols, SLOT), jnp.bfloat16),
+            pltpu.VMEM((rows, KV_HEADS, cols, SLOT), jnp.bfloat16),
             pltpu.VMEM((rows, 16, channels), jnp.float32),
             pltpu.VMEM((rows * cols, channels), jnp.bfloat16),
             pltpu.SemaphoreType.DMA((rows,)),
-            pltpu.SemaphoreType.DMA((rows * KV_HEADS,)),
+            pltpu.SemaphoreType.DMA((2 * KV_HEADS,)),
         ],
         compiler_params=pltpu.CompilerParams(vmem_limit_bytes=VMEM_LIMIT),
         cost_estimate=pl.CostEstimate(
@@ -343,11 +380,8 @@
     west = lon < columns // 2
     first, last = lat == 0, lat == bands - 1
 
-    def rim(west_north):
-        start = jnp.where(west == west_north, 0, rows - 2)
-        return lax.dynamic_slice_in_dim(u, start, 2, axis=0)
-
-    rim_a, rim_b, u = lax.optimization_barrier((rim(True), rim(False), u))
+    rim_a, rim_b = rims(west.astype(jnp.int32)[None], u)
+    rim_a, rim_b, u = lax.optimization_barrier((rim_a, rim_b, u))
     a = lax.ppermute(rim_a, ("lat", "lon"), meridian_pairs(bands, columns, True))
     b = lax.ppermute(rim_b, ("lat", "lon"), meridian_pairs(bands, columns, False))
 
@@ -373,7 +407,7 @@
         [query_weight[:, g * QW : (g + 1) * QW] for g in range(KV_HEADS)],
         key_value_weight,
     )
-    circle = lax.all_to_all(slots, "lon", 0, 0, tiled=True)
+    circle = lax.all_to_all(slots.reshape(rows * KV_HEADS, cols, SLOT), "lon", 0, 0, tiled=True)
     displaced = lax.ppermute(
         head_tile[:, :MARGIN], "lon", [(j, (j + 1) % columns) for j in range(columns)]
     )

time: 78.7 us -> 78.5 us (level)
  waiting for transfers between devices: 23.4 us -> 25.2 us
  other arithmetic: 1.36 us -> 0.32 us
  local copies, waits for them, and re-layouts: 3.75 us -> 2.88 us
    ppermute x1, waiting for transfers between devices: 5.05 us -> 6.93 us  [local(): lax.ppermute(rim_a, ('lat', 'lon'), meridian_pairs(bands, columns, True))]
    dynamic_slice x1 -> x0, local copies, waits for them, and re-layouts: 1.07 us -> none  [rim(): return lax.dynamic_slice_in_dim(u, start, 2, axis=0)]
    convert_element_type x1, other arithmetic: 1.15 us -> 0.11 us  [local(): u.astype(jnp.float32)]
    unnamed x10 -> x12, local copies, waits for them, and re-layouts: 0.05 us -> 1.09 us
    slice x1, local copies, waits for them, and re-layouts: 0.85 us -> 0.01 us  [local(): ea, eb, eu = (a[:, :2 * MARGIN], b[:, :2 * MARGIN], u[:, :2 * MARGIN])]
  transfers between devices with their start and end apart: 5 -> 5, of which waited for: 5 -> 5; matrix products, arithmetic and copies ran while one was open for 5% -> 3% of each run, Pallas kernels for 3% -> 3%
where the time goes in v4:
time: 78.5 us; the launch traced here: 77.2 us
  waiting for transfers between devices  25.2 us (32%)
  starting transfers between devices  21.4 us (27%)
  blocking collectives  14.9 us (19%)
  Pallas kernels  11.7 us (15%)
  local copies, waits for them, and re-layouts  2.88 us (4%)
  between operations  0.8 us (1%)
    all_to_all x1, blocking collectives, local(): back = lax.all_to_all(back, 'lon', 0, 0, tiled=True)  14.9 us
    ppermute x1, waiting for transfers between devices, local(): lax.ppermute(rim_b, ('lat', 'lon'), meridian_pairs(bands, columns, False))  7.02 us
    ppermute x1, waiting for transfers between devices, local(): lax.ppermute(rim_a, ('lat', 'lon'), meridian_pairs(bands, columns, True))  6.93 us
    all_to_all x1, starting transfers between devices, local(): lax.all_to_all(slots.reshape(rows * KV_HEADS, cols, SLOT), 'lon', 0, 0, t...  6.88 us
    ppermute x1, waiting for transfers between devices, local(): lax.ppermute(head_tile[:, :MARGIN], 'lon', [(j, (j + 1) % columns) for j...  5.73 us
    ppermute x1, starting transfers between devices, local(): lax.ppermute(rim_a, ('lat', 'lon'), meridian_pairs(bands, columns, True))  5.65 us
    all_to_all x1, waiting for transfers between devices, local(): lax.all_to_all(slots.reshape(rows * KV_HEADS, cols, SLOT), 'lon', 0, 0, t...  5.2 us
    pallas_call x1, Pallas kernels, attention(): pl.pallas_call(attention_kernel, out_shape=jax.ShapeDtypeStruct((blocks,...  5.13 us
  transfers between devices with their start and end apart: 5, of which 5 were waited for; matrix products, arithmetic and copies ran while one was open for 3% of the time, Pallas kernels for 3%

profile of v4, /device:TPU:1, one launch (start us, length us, event | category | flops | bytes accessed | tf_op | source)
XLA Modules:
  0.0 77.2 jit_solution(3301951494809402503)
XLA Ops:
  0.6 0.0 copy-start
  0.6 1.0 %copy-done = bf16[1,4,64,1024]{3,2,1,0:T(8,128)(2,1)S(1)} copy-done((bf16[1,4,64,1024]{3,2,1,0:T(8,128)(2,1)S(1)}, bf16[1,4,64,1024]{3,2,1,0:T(8,128)(2,1)}, u32[]{:S(2)}) %copy-start) | copy-done | bytes 524312
  1.7 0.0 copy-start.3
  1.7 0.0 copy-start.4
  1.7 0.1 rims.1
  1.7 5.7 %collective-permute-start = (bf16[2,64,1024]{2,1,0:T(8,128)(2,1)S(1)}, bf16[2,64,1024]{2,1,0:T(8,128)(2,1)S(1)}, u32[]{:S(2)}, u32[]{:S(2)}) collective-permute-start(bf16[2,64,1024]{2,1,0:T(8,128)(2,1)S(1)} %get-tuple-element.19), channel_id=1, source_target_pairs={{0,8},{1,9},{2,10},{3,11},{4,12},{5,13},{6,14},{7,15},{8,24},{9,25... | collective-permute-start | bytes 786440 | tf_op jit(solution)/shard_map/ppermute | solution.py:385
  7.4 1.9 %collective-permute-start.1 = (bf16[2,64,1024]{2,1,0:T(8,128)(2,1)S(1)}, bf16[2,64,1024]{2,1,0:T(8,128)(2,1)S(1)}, u32[]{:S(2)}, u32[]{:S(2)}) collective-permute-start(bf16[2,64,1024]{2,1,0:T(8,128)(2,1)S(1)} %get-tuple-element.20), channel_id=1, source_target_pairs={{0,16},{1,17},{2,18},{3,19},{4,20},{5,21},{6,22},{7,23},{8,0},{9,1... | collective-permute-start | bytes 786440 | tf_op jit(solution)/shard_map/ppermute | solution.py:386
  9.4 0.1 convert_element_type.12.u_ref
  9.5 0.0 copy-done.3
  9.6 0.0 copy-done.4
  9.6 0.0 copy-start.1
  9.6 0.0 copy-start.2
  9.6 1.8 %fusion = (bf16[1024,256]{1,0:T(8,128)(2,1)S(1)}, bf16[1024,256]{1,0:T(8,128)(2,1)S(1)}, bf16[1024,256]{1,0:T(8,128)(2,1)S(1)}, bf16[1024,256]{1,0:T(8,128)(2,1)S(1)}) fusion(bf16[1024,1024]{1,0:T(8,128)(2,1)} %param.10), kind=kLoop, calls=%fused_computation.7 | loop fusion | bytes 4194304 | tf_op jit(solution)/shard_map/slice | solution.py:407
  11.4 6.9 %collective-permute-done.a_ref = bf16[2,64,1024]{2,1,0:T(8,128)(2,1)S(1)} collective-permute-done((bf16[2,64,1024]{2,1,0:T(8,128)(2,1)S(1)}, bf16[2,64,1024]{2,1,0:T(8,128)(2,1)S(1)}, u32[]{:S(2)}, u32[]{:S(2)}) %collective-permute-start) | collective-permute-done | bytes 262176 | tf_op jit(solution)/shard_map/ppermute | solution.py:385
  18.3 7.0 %collective-permute-done.1.b_ref = bf16[2,64,1024]{2,1,0:T(8,128)(2,1)S(1)} collective-permute-done((bf16[2,64,1024]{2,1,0:T(8,128)(2,1)S(1)}, bf16[2,64,1024]{2,1,0:T(8,128)(2,1)S(1)}, u32[]{:S(2)}, u32[]{:S(2)}) %collective-permute-start.1) | collective-permute-done | bytes 262176 | tf_op jit(solution)/shard_map/ppermute | solution.py:386
  25.4 0.1 pad_maximum_fusion
  25.4 3.5 %collective-permute-start.2 = (bf16[8,4,1024]{2,1,0:T(4,128)(2,1)S(1)}, bf16[8,4,1024]{2,1,0:T(4,128)(2,1)S(1)}, u32[]{:S(2)}, u32[]{:S(2)}) collective-permute-start(bf16[8,4,1024]{2,1,0:T(4,128)(2,1)S(1)} %pad_maximum_fusion), channel_id=1, source_target_pairs={{0,15},{1,0},{2,1},{3,2},{4,3},{5,4},{6,5},{7,6},{8,7},{9,8},{10,9... | collective-permute-start | bytes 196616 | tf_op jit(solution)/shard_map/ppermute | solution.py:392
  28.9 0.1 add_convert_fusion.flag_ref
  29.0 2.6 %inner.1 = (bf16[4,64,1024]{2,1,0:T(8,128)(2,1)S(1)}, bf16[8,8,1024]{2,1,0:T(8,128)(2,1)S(1)}) custom-call(f32[8]{0:T(128)S(1)} %sine_abs_fusion.c_ref, s32[3]{0:T(128)S(1)} %add_convert_fusion.flag_ref, f32[4,64,1024]{2,1,0:T(8,128)S(1)} %convert_element_type.12.u_ref, bf16[2,64,1024]{2,1,0:T(8,128)(2,1)S(1)} %collective-permute-done.a_ref, ...), custom_call_target="tpu_custom_call" | custom-call | flops 10485760 | bytes 8388608 | tf_op jit(solution)/shard_map/inner/pallas_call | solution.py:143
  31.6 0.4 collective-permute-done.2.edge_ref
  31.9 0.0 copy-done.1
  31.9 0.0 copy-done.2
  31.9 3.0 %project.1 = (bf16[4,64,1024]{2,1,0:T(8,128)(2,1)}, bf16[4,4,64,384]{3,2,1,0:T(8,128)(2,1)}, bf16[4,16,1024]{2,1,0:T(8,128)(2,1)S(1)}) custom-call(f32[8]{0:T(128)S(1)} %sine_abs_fusion.c_ref, bf16[8,8,1024]{2,1,0:T(8,128)(2,1)S(1)} %get-tuple-element.21.side_ref, bf16[8,4,1024]{2,1,0:T(4,128)(2,1)S(1)} %collective-permute-done.2.edge_ref, ...), custom_call_target="tpu_custom_call" | custom-call | flops 805306368 | bytes 6291456 | tf_op jit(solution)/shard_map/project/pallas_call | solution.py:260
  35.0 6.9 %all-to-all-start = ((bf16[16,64,384]{2,1,0:T(8,128)(2,1)}), bf16[16,64,384]{2,1,0:T(8,128)(2,1)S(1)}, u32[]{:S(2)}, u32[]{:S(2)}) async-start(bf16[16,64,384]{2,1,0:T(8,128)(2,1)} %bitcast.5), calls=%async_computation | async-start | bytes 1572864 | tf_op jit(solution)/shard_map/all_to_all | solution.py:410
  41.9 3.5 %collective-permute-start.3 = (bf16[4,2,1024]{2,1,0:T(2,128)(2,1)S(1)}, bf16[4,2,1024]{2,1,0:T(2,128)(2,1)S(1)}, u32[]{:S(2)}, u32[]{:S(2)}) collective-permute-start(bf16[4,2,1024]{2,1,0:T(2,128)(2,1)S(1)} %slice.31), channel_id=1, source_target_pairs={{0,1},{1,2},{2,3},{3,4},{4,5},{5,6},{6,7},{7,8},{8,9},{9,10},{10,1... | collective-permute-start | bytes 49160 | tf_op jit(solution)/shard_map/ppermute | solution.py:411
  45.4 5.7 %collective-permute-done.3.displaced_ref = bf16[4,2,1024]{2,1,0:T(2,128)(2,1)S(1)} collective-permute-done((bf16[4,2,1024]{2,1,0:T(2,128)(2,1)S(1)}, bf16[4,2,1024]{2,1,0:T(2,128)(2,1)S(1)}, u32[]{:S(2)}, u32[]{:S(2)}) %collective-permute-start.3) | collective-permute-done | bytes 16416 | tf_op jit(solution)/shard_map/ppermute | solution.py:411
  51.1 5.2 %all-to-all-done = bf16[16,64,384]{2,1,0:T(8,128)(2,1)S(1)} async-done(((bf16[16,64,384]{2,1,0:T(8,128)(2,1)}), bf16[16,64,384]{2,1,0:T(8,128)(2,1)S(1)}, u32[]{:S(2)}, u32[]{:S(2)}) %all-to-all-start) | async-done | bytes 786464 | tf_op jit(solution)/shard_map/all_to_all | solution.py:410
  56.3 5.1 %attention.1 = bf16[16,64,256]{2,1,0:T(8,128)(2,1)S(1)} custom-call(bf16[1024,384]{1,0:T(8,128)(2,1)S(1)} %bitcast.12), custom_call_target="tpu_custom_call" | custom-call | flops 1073741824 | bytes 1310720 | tf_op jit(solution)/shard_map/attention/pallas_call | solution.py:319
  61.5 14.9 %all_to_all.10.x_ref = bf16[16,64,256]{2,1,0:T(8,128)(2,1)S(1)} all-to-all(bf16[16,64,256]{2,1,0:T(8,128)(2,1)S(1)} %attention.1), channel_id=1, replica_groups=mesh['lat'=32,'lon'=16] {'lon'}, dimensions={0} | all-to-all | bytes 1048576 | tf_op jit(solution)/shard_map/all_to_all | solution.py:416
  76.3 0.9 %gather_heads.1 = (bf16[4,64,1024]{2,1,0:T(8,128)(2,1)}, bf16[4,64,1024]{2,1,0:T(8,128)(2,1)}) custom-call(bf16[16,64,256]{2,1,0:T(8,128)(2,1)S(1)} %all_to_all.10.x_ref, bf16[4,16,1024]{2,1,0:T(8,128)(2,1)S(1)} %get-tuple-element.24.head_ref, bf16[4,2,1024]{2,1,0:T(2,128)(2,1)S(1)} %collective-permute-done.3.displaced_ref, ...), custom_call_target="tpu_custom_call", output_to_operand_aliasing={{1}: (3, {})} | custom-call | tf_op jit(solution)/shard_map/gather_heads/pallas_call | solution.py:358
  (7 shorter events, 0.1 us)
Async XLA Ops:
  0.6 1.0 %copy-start = (bf16[1,4,64,1024]{3,2,1,0:T(8,128)(2,1)S(1)}, bf16[1,4,64,1024]{3,2,1,0:T(8,128)(2,1)}, u32[]{:S(2)}) copy-start(bf16[1,4,64,1024]{3,2,1,0:T(8,128)(2,1)} %param.6) | copy-start | bytes 1572868
  1.7 7.8 %copy-start.3 = (f32[2,3,1024]{2,0,1:T(2,128)S(1)}, f32[2,3,1024]{2,0,1:T(2,128)}, u32[]{:S(2)}) copy-start(f32[2,3,1024]{2,0,1:T(2,128)} %param.7) | copy-start | bytes 73732
  1.7 7.9 %copy-start.4 = (f32[2,3,1024]{2,0,1:T(2,128)S(1)}, f32[2,3,1024]{2,0,1:T(2,128)}, u32[]{:S(2)}) copy-start(f32[2,3,1024]{2,0,1:T(2,128)} %param.8) | copy-start | bytes 73732
  1.7 16.6 %collective-permute-start = (bf16[2,64,1024]{2,1,0:T(8,128)(2,1)S(1)}, bf16[2,64,1024]{2,1,0:T(8,128)(2,1)S(1)}, u32[]{:S(2)}, u32[]{:S(2)}) collective-permute-start(bf16[2,64,1024]{2,1,0:T(8,128)(2,1)S(1)} %get-tuple-element.19), channel_id=1, source_target_pairs={{0,8},{1,9},{2,10},{3,11},{4,12},{5,13},{6,14},{7,15},{8,24},{9,25... | collective-permute-start | bytes 786440 | tf_op jit(solution)/shard_map/ppermute | solution.py:385
  7.4 17.9 %collective-permute-start.1 = (bf16[2,64,1024]{2,1,0:T(8,128)(2,1)S(1)}, bf16[2,64,1024]{2,1,0:T(8,128)(2,1)S(1)}, u32[]{:S(2)}, u32[]{:S(2)}) collective-permute-start(bf16[2,64,1024]{2,1,0:T(8,128)(2,1)S(1)} %get-tuple-element.20), channel_id=1, source_target_pairs={{0,16},{1,17},{2,18},{3,19},{4,20},{5,21},{6,22},{7,23},{8,0},{9,1... | collective-permute-start | bytes 786440 | tf_op jit(solution)/shard_map/ppermute | solution.py:386
  9.6 22.3 %copy-start.1 = (bf16[1024,512]{1,0:T(8,128)(2,1)S(1)}, bf16[1024,512]{1,0:T(8,128)(2,1)}, u32[]{:S(2)}) copy-start(bf16[1024,512]{1,0:T(8,128)(2,1)} %wkv.1) | copy-start | bytes 3145732
  9.6 22.3 %copy-start.2 = (f32[1024]{0:T(1024)S(1)}, f32[1024]{0:T(1024)}, u32[]{:S(2)}) copy-start(f32[1024]{0:T(1024)} %param.9) | copy-start | bytes 12292
  25.4 6.5 %collective-permute-start.2 = (bf16[8,4,1024]{2,1,0:T(4,128)(2,1)S(1)}, bf16[8,4,1024]{2,1,0:T(4,128)(2,1)S(1)}, u32[]{:S(2)}, u32[]{:S(2)}) collective-permute-start(bf16[8,4,1024]{2,1,0:T(4,128)(2,1)S(1)} %pad_maximum_fusion), channel_id=1, source_target_pairs={{0,15},{1,0},{2,1},{3,2},{4,3},{5,4},{6,5},{7,6},{8,7},{9,8},{10,9... | collective-permute-start | bytes 196616 | tf_op jit(solution)/shard_map/ppermute | solution.py:392
  35.0 21.4 %all-to-all-start = ((bf16[16,64,384]{2,1,0:T(8,128)(2,1)}), bf16[16,64,384]{2,1,0:T(8,128)(2,1)S(1)}, u32[]{:S(2)}, u32[]{:S(2)}) async-start(bf16[16,64,384]{2,1,0:T(8,128)(2,1)} %bitcast.5), calls=%async_computation | async-start | bytes 1572864 | tf_op jit(solution)/shard_map/all_to_all | solution.py:410
  41.9 9.3 %collective-permute-start.3 = (bf16[4,2,1024]{2,1,0:T(2,128)(2,1)S(1)}, bf16[4,2,1024]{2,1,0:T(2,128)(2,1)S(1)}, u32[]{:S(2)}, u32[]{:S(2)}) collective-permute-start(bf16[4,2,1024]{2,1,0:T(2,128)(2,1)S(1)} %slice.31), channel_id=1, source_target_pairs={{0,1},{1,2},{2,3},{3,4},{4,5},{5,6},{6,7},{7,8},{8,9},{9,10},{10,1... | collective-permute-start | bytes 49160 | tf_op jit(solution)/shard_map/ppermute | solution.py:411

commit v5 on v4

--- a/solution.py
+++ b/solution.py
@@ -75,15 +75,18 @@
     return raw + t[1] + pltpu.roll(t[0], 1, 0) + pltpu.roll(t[2], raw.shape[0] - 1, 0)
 
 
-def two_stencils(row, count, c_ref, one_ref, two_ref, lanes, store):
+def two_stencils(row, count, c_ref, one_ref, two_ref, lanes, store, known=None):
     raw = [row(0), row(1)]
     scaled = [raw[0] * c_ref[0], raw[1] * c_ref[1]]
     after, after_scaled = [None], [None]
     for r in range(2, count + 4):
         raw.append(row(r))
         scaled.append(raw[r] * c_ref[r])
-        v = add_stencil(scaled[r - 2], scaled[r - 1], scaled[r], raw[r - 1], one_ref, lanes)
-        v = v.astype(jnp.bfloat16).astype(jnp.float32)
+        if known is not None and 4 <= r < count + 2:
+            v = known(r - 4)
+        else:
+            v = add_stencil(scaled[r - 2], scaled[r - 1], scaled[r], raw[r - 1], one_ref, lanes)
+            v = v.astype(jnp.bfloat16).astype(jnp.float32)
         after.append(v)
         after_scaled.append(v * c_ref[r - 1])
         if r >= 4:
@@ -100,7 +103,40 @@
             )
 
 
-def inner_kernel(c_ref, flag_ref, u_ref, a_ref, b_ref, one_ref, two_ref, mixed_ref, side_ref):
+def own_rows_kernel(c_ref, u_ref, one_ref, known_ref):
+    rows, _, channels = u_ref.shape
+
+    def chunk(n, _):
+        lanes = pl.ds(pl.multiple_of(n * LANES, LANES), LANES)
+        raw = [u_ref[r, :, lanes] for r in range(rows)]
+        scaled = [raw[r] * c_ref[r + 2] for r in range(rows)]
+        for r in range(1, rows - 1):
+            v = add_stencil(scaled[r - 1], scaled[r], scaled[r + 1], raw[r], one_ref, lanes)
+            known_ref[r - 1, :, lanes] = v.astype(jnp.bfloat16)
+        return 0
+
+    lax.fori_loop(0, channels // LANES, chunk, 0)
+
+
+def own_rows(c, u, one):
+    rows, cols, channels = u.shape
+    vmem, smem = pl.BlockSpec(memory_space=pltpu.VMEM), pl.BlockSpec(memory_space=pltpu.SMEM)
+    return pl.pallas_call(
+        own_rows_kernel,
+        out_shape=jax.ShapeDtypeStruct((rows - 2, cols, channels), jnp.bfloat16),
+        in_specs=[smem, vmem, vmem],
+        out_specs=vmem,
+        compiler_params=pltpu.CompilerParams(vmem_limit_bytes=VMEM_LIMIT),
+        cost_estimate=pl.CostEstimate(
+            flops=8 * rows * cols * channels, bytes_accessed=1024 * 1024, transcendentals=0
+        ),
+        name="own_rows",
+    )(c, u, one)
+
+
+def inner_kernel(
+    c_ref, flag_ref, u_ref, known_ref, a_ref, b_ref, one_ref, two_ref, mixed_ref, side_ref
+):
     rows, cols, channels = u_ref.shape
     west = flag_ref[0] == 1
     north, south = flag_ref[1], flag_ref[2]
@@ -131,13 +167,16 @@
         def store(r, v):
             mixed_ref[r, :, lanes] = v.astype(jnp.bfloat16)
 
-        two_stencils(row, rows, c_ref, one_ref, two_ref, lanes, store)
+        def known(r):
+            return known_ref[r, :, lanes].astype(jnp.float32)
+
+        two_stencils(row, rows, c_ref, one_ref, two_ref, lanes, store, known)
         return 0
 
     lax.fori_loop(0, channels // LANES, chunk, 0)
 
 
-def inner(c, flags, u, a, b, one, two):
+def inner(c, flags, u, known, a, b, one, two):
     rows, cols, channels = u.shape
     vmem, smem = pl.BlockSpec(memory_space=pltpu.VMEM), pl.BlockSpec(memory_space=pltpu.SMEM)
     return pl.pallas_call(
@@ -146,14 +185,14 @@
             jax.ShapeDtypeStruct((rows, cols, channels), jnp.bfloat16),
             jax.ShapeDtypeStruct((rows + 4, 8, channels), jnp.bfloat16),
         ),
-        in_specs=[smem, smem] + [vmem] * 5,
+        in_specs=[smem, smem] + [vmem] * 6,
         out_specs=(vmem, vmem),
         compiler_params=pltpu.CompilerParams(vmem_limit_bytes=VMEM_LIMIT),
         cost_estimate=pl.CostEstimate(
             flops=40 * rows * cols * channels, bytes_accessed=8 * 1024 * 1024, transcendentals=0
         ),
         name="inner",
-    )(c, flags, u, a, b, one, two)
+    )(c, flags, u, known, a, b, one, two)
 
 
 def project_kernel(
@@ -394,8 +433,11 @@
         "lon",
         [(j, (j - 1) % columns) for j in range(columns)],
     )
+    wide = u.astype(jnp.float32)
     flags = jnp.stack([west, first, last]).astype(jnp.int32)
-    mixed_inner, side = inner(c, flags, u.astype(jnp.float32), a, b, stencil_one, stencil_two)
+    mixed_inner, side = inner(
+        c, flags, wide, own_rows(c, wide, stencil_one), a, b, stencil_one, stencil_two
+    )
     mixed_field, slots, head_tile = project(
         c,
         side,

time: 78.5 us -> 78.5 us (level)
    pallas_call x0 -> x1, Pallas kernels: none -> 0.97 us  [own_rows(): pl.pallas_call(own_rows_kernel, out_shape=jax.ShapeDtypeStruct((rows - 2,...]
    ppermute x1, waiting for transfers between devices: 6.93 us -> 6.03 us  [local(): lax.ppermute(rim_a, ('lat', 'lon'), meridian_pairs(bands, columns, True))]
  transfers between devices with their start and end apart: 5 -> 5, of which waited for: 5 -> 5; matrix products, arithmetic and copies ran while one was open for 3% -> 3% of each run, Pallas kernels for 3% -> 4%
where the time goes in v5:
time: 78.5 us; the launch traced here: 77.2 us
  waiting for transfers between devices  24.7 us (31%)
  starting transfers between devices  21.4 us (27%)
  blocking collectives  14.9 us (19%)
  Pallas kernels  12.3 us (16%)
  local copies, waits for them, and re-layouts  2.79 us (4%)
  between operations  0.81 us (1%)
    all_to_all x1, blocking collectives, local(): back = lax.all_to_all(back, 'lon', 0, 0, tiled=True)  14.9 us
    ppermute x1, waiting for transfers between devices, local(): lax.ppermute(rim_b, ('lat', 'lon'), meridian_pairs(bands, columns, False))  7.02 us
    all_to_all x1, starting transfers between devices, local(): lax.all_to_all(slots.reshape(rows * KV_HEADS, cols, SLOT), 'lon', 0, 0, t...  6.88 us
    ppermute x1, waiting for transfers between devices, local(): lax.ppermute(rim_a, ('lat', 'lon'), meridian_pairs(bands, columns, True))  6.03 us
    ppermute x1, waiting for transfers between devices, local(): lax.ppermute(head_tile[:, :MARGIN], 'lon', [(j, (j + 1) % columns) for j...  5.73 us
    ppermute x1, starting transfers between devices, local(): lax.ppermute(rim_a, ('lat', 'lon'), meridian_pairs(bands, columns, True))  5.65 us
    all_to_all x1, waiting for transfers between devices, local(): lax.all_to_all(slots.reshape(rows * KV_HEADS, cols, SLOT), 'lon', 0, 0, t...  5.2 us
    pallas_call x1, Pallas kernels, attention(): pl.pallas_call(attention_kernel, out_shape=jax.ShapeDtypeStruct((blocks,...  5.13 us
  transfers between devices with their start and end apart: 5, of which 5 were waited for; matrix products, arithmetic and copies ran while one was open for 3% of the time, Pallas kernels for 4%

profile of v5, /device:TPU:1, one launch (start us, length us, event | category | flops | bytes accessed | tf_op | source)
XLA Modules:
  0.0 77.2 jit_solution(15291877626368542925)
XLA Ops:
  0.6 0.0 copy-start
  0.6 1.0 %copy-done = bf16[1,4,64,1024]{3,2,1,0:T(8,128)(2,1)S(1)} copy-done((bf16[1,4,64,1024]{3,2,1,0:T(8,128)(2,1)S(1)}, bf16[1,4,64,1024]{3,2,1,0:T(8,128)(2,1)}, u32[]{:S(2)}) %copy-start) | copy-done | bytes 524312
  1.7 0.0 copy-start.3
  1.7 0.0 copy-start.4
  1.7 0.1 rims.1
  1.7 5.7 %collective-permute-start = (bf16[2,64,1024]{2,1,0:T(8,128)(2,1)S(1)}, bf16[2,64,1024]{2,1,0:T(8,128)(2,1)S(1)}, u32[]{:S(2)}, u32[]{:S(2)}) collective-permute-start(bf16[2,64,1024]{2,1,0:T(8,128)(2,1)S(1)} %get-tuple-element.19), channel_id=1, source_target_pairs={{0,8},{1,9},{2,10},{3,11},{4,12},{5,13},{6,14},{7,15},{8,24},{9,25... | collective-permute-start | bytes 786440 | tf_op jit(solution)/shard_map/ppermute | solution.py:424
  7.4 1.9 %collective-permute-start.1 = (bf16[2,64,1024]{2,1,0:T(8,128)(2,1)S(1)}, bf16[2,64,1024]{2,1,0:T(8,128)(2,1)S(1)}, u32[]{:S(2)}, u32[]{:S(2)}) collective-permute-start(bf16[2,64,1024]{2,1,0:T(8,128)(2,1)S(1)} %get-tuple-element.20), channel_id=1, source_target_pairs={{0,16},{1,17},{2,18},{3,19},{4,20},{5,21},{6,22},{7,23},{8,0},{9,1... | collective-permute-start | bytes 786440 | tf_op jit(solution)/shard_map/ppermute | solution.py:425
  9.4 0.1 convert_element_type.12.u_ref
  9.5 0.0 copy-done.3
  9.6 0.0 copy-done.4
  9.6 1.0 %own_rows.1.known_ref = bf16[2,64,1024]{2,1,0:T(8,128)(2,1)S(1)} custom-call(f32[8]{0:T(128)S(1)} %sine_abs_fusion.c_ref, f32[4,64,1024]{2,1,0:T(8,128)S(1)} %convert_element_type.12.u_ref, f32[2,3,1024]{2,1,0:T(4,128)S(1)} %copy.9.one_ref), custom_call_target="tpu_custom_call" | custom-call | flops 2097152 | bytes 1048576 | tf_op jit(solution)/shard_map/own_rows/pallas_call | solution.py:124
  10.6 1.7 %fusion = (bf16[1024,256]{1,0:T(8,128)(2,1)S(1)}, bf16[1024,256]{1,0:T(8,128)(2,1)S(1)}, bf16[1024,256]{1,0:T(8,128)(2,1)S(1)}, bf16[1024,256]{1,0:T(8,128)(2,1)S(1)}) fusion(bf16[1024,1024]{1,0:T(8,128)(2,1)} %param.10), kind=kLoop, calls=%fused_computation.7 | loop fusion | bytes 4194304 | tf_op jit(solution)/shard_map/slice | solution.py:449
  12.3 0.0 copy-start.1
  12.3 0.0 copy-start.2
  12.3 6.0 %collective-permute-done.a_ref = bf16[2,64,1024]{2,1,0:T(8,128)(2,1)S(1)} collective-permute-done((bf16[2,64,1024]{2,1,0:T(8,128)(2,1)S(1)}, bf16[2,64,1024]{2,1,0:T(8,128)(2,1)S(1)}, u32[]{:S(2)}, u32[]{:S(2)}) %collective-permute-start) | collective-permute-done | bytes 262176 | tf_op jit(solution)/shard_map/ppermute | solution.py:424
  18.3 7.0 %collective-permute-done.1.b_ref = bf16[2,64,1024]{2,1,0:T(8,128)(2,1)S(1)} collective-permute-done((bf16[2,64,1024]{2,1,0:T(8,128)(2,1)S(1)}, bf16[2,64,1024]{2,1,0:T(8,128)(2,1)S(1)}, u32[]{:S(2)}, u32[]{:S(2)}) %collective-permute-start.1) | collective-permute-done | bytes 262176 | tf_op jit(solution)/shard_map/ppermute | solution.py:425
  25.4 0.1 pad_maximum_fusion
  25.4 3.5 %collective-permute-start.2 = (bf16[8,4,1024]{2,1,0:T(4,128)(2,1)S(1)}, bf16[8,4,1024]{2,1,0:T(4,128)(2,1)S(1)}, u32[]{:S(2)}, u32[]{:S(2)}) collective-permute-start(bf16[8,4,1024]{2,1,0:T(4,128)(2,1)S(1)} %pad_maximum_fusion), channel_id=1, source_target_pairs={{0,15},{1,0},{2,1},{3,2},{4,3},{5,4},{6,5},{7,6},{8,7},{9,8},{10,9... | collective-permute-start | bytes 196616 | tf_op jit(solution)/shard_map/ppermute | solution.py:431
  28.9 0.1 add_convert_fusion.flag_ref
  29.0 2.3 %inner.1 = (bf16[4,64,1024]{2,1,0:T(8,128)(2,1)S(1)}, bf16[8,8,1024]{2,1,0:T(8,128)(2,1)S(1)}) custom-call(f32[8]{0:T(128)S(1)} %sine_abs_fusion.c_ref, s32[3]{0:T(128)S(1)} %add_convert_fusion.flag_ref, f32[4,64,1024]{2,1,0:T(8,128)S(1)} %convert_element_type.12.u_ref, bf16[2,64,1024]{2,1,0:T(8,128)(2,1)S(1)} %own_rows.1.known_ref, ...), custom_call_target="tpu_custom_call" | custom-call | flops 10485760 | bytes 8388608 | tf_op jit(solution)/shard_map/inner/pallas_call | solution.py:182
  31.2 0.7 collective-permute-done.2.edge_ref
  31.9 0.0 copy-done.1
  31.9 0.0 copy-done.2
  31.9 3.0 %project.1 = (bf16[4,64,1024]{2,1,0:T(8,128)(2,1)}, bf16[4,4,64,384]{3,2,1,0:T(8,128)(2,1)}, bf16[4,16,1024]{2,1,0:T(8,128)(2,1)S(1)}) custom-call(f32[8]{0:T(128)S(1)} %sine_abs_fusion.c_ref, bf16[8,8,1024]{2,1,0:T(8,128)(2,1)S(1)} %get-tuple-element.21.side_ref, bf16[8,4,1024]{2,1,0:T(4,128)(2,1)S(1)} %collective-permute-done.2.edge_ref, ...), custom_call_target="tpu_custom_call" | custom-call | flops 805306368 | bytes 6291456 | tf_op jit(solution)/shard_map/project/pallas_call | solution.py:299
  34.9 6.9 %all-to-all-start = ((bf16[16,64,384]{2,1,0:T(8,128)(2,1)}), bf16[16,64,384]{2,1,0:T(8,128)(2,1)S(1)}, u32[]{:S(2)}, u32[]{:S(2)}) async-start(bf16[16,64,384]{2,1,0:T(8,128)(2,1)} %bitcast.5), calls=%async_computation | async-start | bytes 1572864 | tf_op jit(solution)/shard_map/all_to_all | solution.py:452
  41.8 3.5 %collective-permute-start.3 = (bf16[4,2,1024]{2,1,0:T(2,128)(2,1)S(1)}, bf16[4,2,1024]{2,1,0:T(2,128)(2,1)S(1)}, u32[]{:S(2)}, u32[]{:S(2)}) collective-permute-start(bf16[4,2,1024]{2,1,0:T(2,128)(2,1)S(1)} %slice.31), channel_id=1, source_target_pairs={{0,1},{1,2},{2,3},{3,4},{4,5},{5,6},{6,7},{7,8},{8,9},{9,10},{10,1... | collective-permute-start | bytes 49160 | tf_op jit(solution)/shard_map/ppermute | solution.py:453
  45.4 5.7 %collective-permute-done.3.displaced_ref = bf16[4,2,1024]{2,1,0:T(2,128)(2,1)S(1)} collective-permute-done((bf16[4,2,1024]{2,1,0:T(2,128)(2,1)S(1)}, bf16[4,2,1024]{2,1,0:T(2,128)(2,1)S(1)}, u32[]{:S(2)}, u32[]{:S(2)}) %collective-permute-start.3) | collective-permute-done | bytes 16416 | tf_op jit(solution)/shard_map/ppermute | solution.py:453
  51.1 5.2 %all-to-all-done = bf16[16,64,384]{2,1,0:T(8,128)(2,1)S(1)} async-done(((bf16[16,64,384]{2,1,0:T(8,128)(2,1)}), bf16[16,64,384]{2,1,0:T(8,128)(2,1)S(1)}, u32[]{:S(2)}, u32[]{:S(2)}) %all-to-all-start) | async-done | bytes 786464 | tf_op jit(solution)/shard_map/all_to_all | solution.py:452
  56.3 5.1 %attention.1 = bf16[16,64,256]{2,1,0:T(8,128)(2,1)S(1)} custom-call(bf16[1024,384]{1,0:T(8,128)(2,1)S(1)} %bitcast.12), custom_call_target="tpu_custom_call" | custom-call | flops 1073741824 | bytes 1310720 | tf_op jit(solution)/shard_map/attention/pallas_call | solution.py:358
  61.5 14.9 %all_to_all.10.x_ref = bf16[16,64,256]{2,1,0:T(8,128)(2,1)S(1)} all-to-all(bf16[16,64,256]{2,1,0:T(8,128)(2,1)S(1)} %attention.1), channel_id=1, replica_groups=mesh['lat'=32,'lon'=16] {'lon'}, dimensions={0} | all-to-all | bytes 1048576 | tf_op jit(solution)/shard_map/all_to_all | solution.py:458
  76.3 0.9 %gather_heads.1 = (bf16[4,64,1024]{2,1,0:T(8,128)(2,1)}, bf16[4,64,1024]{2,1,0:T(8,128)(2,1)}) custom-call(bf16[16,64,256]{2,1,0:T(8,128)(2,1)S(1)} %all_to_all.10.x_ref, bf16[4,16,1024]{2,1,0:T(8,128)(2,1)S(1)} %get-tuple-element.24.head_ref, bf16[4,2,1024]{2,1,0:T(2,128)(2,1)S(1)} %collective-permute-done.3.displaced_ref, ...), custom_call_target="tpu_custom_call", output_to_operand_aliasing={{1}: (3, {})} | custom-call | tf_op jit(solution)/shard_map/gather_heads/pallas_call | solution.py:397
  (7 shorter events, 0.1 us)
Async XLA Ops:
  0.6 1.0 %copy-start = (bf16[1,4,64,1024]{3,2,1,0:T(8,128)(2,1)S(1)}, bf16[1,4,64,1024]{3,2,1,0:T(8,128)(2,1)}, u32[]{:S(2)}) copy-start(bf16[1,4,64,1024]{3,2,1,0:T(8,128)(2,1)} %param.6) | copy-start | bytes 1572868
  1.7 7.9 %copy-start.3 = (f32[2,3,1024]{2,0,1:T(2,128)S(1)}, f32[2,3,1024]{2,0,1:T(2,128)}, u32[]{:S(2)}) copy-start(f32[2,3,1024]{2,0,1:T(2,128)} %param.7) | copy-start | bytes 73732
  1.7 7.9 %copy-start.4 = (f32[2,3,1024]{2,0,1:T(2,128)S(1)}, f32[2,3,1024]{2,0,1:T(2,128)}, u32[]{:S(2)}) copy-start(f32[2,3,1024]{2,0,1:T(2,128)} %param.8) | copy-start | bytes 73732
  1.7 16.6 %collective-permute-start = (bf16[2,64,1024]{2,1,0:T(8,128)(2,1)S(1)}, bf16[2,64,1024]{2,1,0:T(8,128)(2,1)S(1)}, u32[]{:S(2)}, u32[]{:S(2)}) collective-permute-start(bf16[2,64,1024]{2,1,0:T(8,128)(2,1)S(1)} %get-tuple-element.19), channel_id=1, source_target_pairs={{0,8},{1,9},{2,10},{3,11},{4,12},{5,13},{6,14},{7,15},{8,24},{9,25... | collective-permute-start | bytes 786440 | tf_op jit(solution)/shard_map/ppermute | solution.py:424
  7.4 17.9 %collective-permute-start.1 = (bf16[2,64,1024]{2,1,0:T(8,128)(2,1)S(1)}, bf16[2,64,1024]{2,1,0:T(8,128)(2,1)S(1)}, u32[]{:S(2)}, u32[]{:S(2)}) collective-permute-start(bf16[2,64,1024]{2,1,0:T(8,128)(2,1)S(1)} %get-tuple-element.20), channel_id=1, source_target_pairs={{0,16},{1,17},{2,18},{3,19},{4,20},{5,21},{6,22},{7,23},{8,0},{9,1... | collective-permute-start | bytes 786440 | tf_op jit(solution)/shard_map/ppermute | solution.py:425
  12.3 19.7 %copy-start.1 = (bf16[1024,512]{1,0:T(8,128)(2,1)S(1)}, bf16[1024,512]{1,0:T(8,128)(2,1)}, u32[]{:S(2)}) copy-start(bf16[1024,512]{1,0:T(8,128)(2,1)} %wkv.1) | copy-start | bytes 3145732
  12.3 19.7 %copy-start.2 = (f32[1024]{0:T(1024)S(1)}, f32[1024]{0:T(1024)}, u32[]{:S(2)}) copy-start(f32[1024]{0:T(1024)} %param.9) | copy-start | bytes 12292
  25.4 6.5 %collective-permute-start.2 = (bf16[8,4,1024]{2,1,0:T(4,128)(2,1)S(1)}, bf16[8,4,1024]{2,1,0:T(4,128)(2,1)S(1)}, u32[]{:S(2)}, u32[]{:S(2)}) collective-permute-start(bf16[8,4,1024]{2,1,0:T(4,128)(2,1)S(1)} %pad_maximum_fusion), channel_id=1, source_target_pairs={{0,15},{1,0},{2,1},{3,2},{4,3},{5,4},{6,5},{7,6},{8,7},{9,8},{10,9... | collective-permute-start | bytes 196616 | tf_op jit(solution)/shard_map/ppermute | solution.py:431
  34.9 21.4 %all-to-all-start = ((bf16[16,64,384]{2,1,0:T(8,128)(2,1)}), bf16[16,64,384]{2,1,0:T(8,128)(2,1)S(1)}, u32[]{:S(2)}, u32[]{:S(2)}) async-start(bf16[16,64,384]{2,1,0:T(8,128)(2,1)} %bitcast.5), calls=%async_computation | async-start | bytes 1572864 | tf_op jit(solution)/shard_map/all_to_all | solution.py:452
  41.8 9.3 %collective-permute-start.3 = (bf16[4,2,1024]{2,1,0:T(2,128)(2,1)S(1)}, bf16[4,2,1024]{2,1,0:T(2,128)(2,1)S(1)}, u32[]{:S(2)}, u32[]{:S(2)}) collective-permute-start(bf16[4,2,1024]{2,1,0:T(2,128)(2,1)S(1)} %slice.31), channel_id=1, source_target_pairs={{0,1},{1,2},{2,3},{3,4},{4,5},{5,6},{6,7},{7,8},{8,9},{9,10},{10,1... | collective-permute-start | bytes 49160 | tf_op jit(solution)/shard_map/ppermute | solution.py:453

commit v6 on v5

--- a/solution.py
+++ b/solution.py
@@ -208,14 +208,12 @@
     wq1,
     wq2,
     wq3,
-    mixed_hbm,
+    mixed_ref,
     slots_hbm,
     head_ref,
-    mixed_ref,
     slots_ref,
     strip,
     normed,
-    sems,
     slot_sems,
 ):
     rows, cols, channels = inner_ref.shape
@@ -259,8 +257,6 @@
             ).astype(jnp.bfloat16)
             mixed_ref[r] = m
             head_ref[r] = m[: 2 * 8]
-            copies.append(pltpu.make_async_copy(mixed_ref.at[r], mixed_hbm.at[r], sems.at[r]))
-            copies[-1].start()
             m = m.astype(jnp.float32)
             mean_square = jnp.sum(m * m, axis=1, keepdims=True) * (1.0 / channels)
             normed[r * cols : (r + 1) * cols, :] = (
@@ -304,13 +300,11 @@
             jax.ShapeDtypeStruct((rows, 16, channels), jnp.bfloat16),
         ),
         in_specs=[smem] + [vmem] * (7 + KV_HEADS),
-        out_specs=(hbm, hbm, vmem),
+        out_specs=(vmem, hbm, vmem),
         scratch_shapes=[
-            pltpu.VMEM((rows, cols, channels), jnp.bfloat16),
             pltpu.VMEM((rows, KV_HEADS, cols, SLOT), jnp.bfloat16),
             pltpu.VMEM((rows, 16, channels), jnp.float32),
             pltpu.VMEM((rows * cols, channels), jnp.bfloat16),
-            pltpu.SemaphoreType.DMA((rows,)),
             pltpu.SemaphoreType.DMA((2 * KV_HEADS,)),
         ],
         compiler_params=pltpu.CompilerParams(vmem_limit_bytes=VMEM_LIMIT),
@@ -323,7 +317,9 @@
     )(c, side, edge, mixed, one, two, gain, wkv, *wq)
 
 
-def attention_kernel(x_ref, o_ref):
+def attention_kernel(x_ref, mixed_ref, o_ref, mixed_hbm, sem):
+    copy = pltpu.make_async_copy(mixed_ref, mixed_hbm, sem)
+    copy.start()
     blocks, cols, _ = o_ref.shape
     n = blocks * cols
     kt = x_ref[:, QW : QW + HEAD_DIM].T
@@ -351,15 +347,23 @@
     moved = lax.broadcasted_iota(jnp.int32, (tile, QW), 0) < MARGIN
     for b in range(blocks):
         o_ref[b, :tile, :] = jnp.where(moved, heads[b - 1], heads[b])
-
-
-def attention(x, blocks):
+    copy.wait()
+
+
+def attention(x, mixed, blocks):
     n = x.shape[0]
     return pl.pallas_call(
         attention_kernel,
-        out_shape=jax.ShapeDtypeStruct((blocks, n // blocks, QW), jnp.bfloat16),
-        in_specs=[pl.BlockSpec(memory_space=pltpu.VMEM)],
-        out_specs=pl.BlockSpec(memory_space=pltpu.VMEM),
+        out_shape=(
+            jax.ShapeDtypeStruct((blocks, n // blocks, QW), jnp.bfloat16),
+            jax.ShapeDtypeStruct(mixed.shape, mixed.dtype),
+        ),
+        in_specs=[pl.BlockSpec(memory_space=pltpu.VMEM)] * 2,
+        out_specs=(
+            pl.BlockSpec(memory_space=pltpu.VMEM),
+            pl.BlockSpec(memory_space=pltpu.HBM),
+        ),
+        scratch_shapes=[pltpu.SemaphoreType.DMA],
         compiler_params=pltpu.CompilerParams(vmem_limit_bytes=VMEM_LIMIT),
         cost_estimate=pl.CostEstimate(
             flops=4 * GROUPS * n * n * HEAD_DIM,
@@ -367,7 +371,7 @@
             transcendentals=GROUPS * n * n,
         ),
         name="attention",
-    )(x)
+    )(x, mixed)
 
 
 def gather_heads_kernel(x_ref, head_ref, displaced_ref, _, o_hbm, mixed_hbm, staged, tile, sems):
@@ -454,7 +458,7 @@
         head_tile[:, :MARGIN], "lon", [(j, (j + 1) % columns) for j in range(columns)]
     )
     circle, displaced = lax.optimization_barrier((circle, displaced))
-    back = attention(circle.reshape(-1, SLOT), columns)
+    back, mixed_field = attention(circle.reshape(-1, SLOT), mixed_field, columns)
     back = lax.all_to_all(back, "lon", 0, 0, tiled=True)
     attended, mixed_field = gather_heads(back, head_tile, displaced, mixed_field)
     return mixed_field[None], attended[None]

time: 78.5 us -> 78.5 us (level)
  no operation moved by 1% of the time
where the time goes in v6:
time: 78.5 us; the launch traced here: 77.2 us
  waiting for transfers between devices  24.7 us (31%)
  starting transfers between devices  21.4 us (27%)
  blocking collectives  14.9 us (19%)
  Pallas kernels  12.3 us (16%)
  local copies, waits for them, and re-layouts  2.79 us (4%)
  between operations  0.82 us (1%)
    all_to_all x1, blocking collectives, local(): back = lax.all_to_all(back, 'lon', 0, 0, tiled=True)  14.9 us
    ppermute x1, waiting for transfers between devices, local(): lax.ppermute(rim_b, ('lat', 'lon'), meridian_pairs(bands, columns, False))  7.02 us
    all_to_all x1, starting transfers between devices, local(): lax.all_to_all(slots.reshape(rows * KV_HEADS, cols, SLOT), 'lon', 0, 0, t...  6.88 us
    ppermute x1, waiting for transfers between devices, local(): lax.ppermute(rim_a, ('lat', 'lon'), meridian_pairs(bands, columns, True))  6.03 us
    ppermute x1, waiting for transfers between devices, local(): lax.ppermute(head_tile[:, :MARGIN], 'lon', [(j, (j + 1) % columns) for j...  5.73 us
    ppermute x1, starting transfers between devices, local(): lax.ppermute(rim_a, ('lat', 'lon'), meridian_pairs(bands, columns, True))  5.65 us
    all_to_all x1, waiting for transfers between devices, local(): lax.all_to_all(slots.reshape(rows * KV_HEADS, cols, SLOT), 'lon', 0, 0, t...  5.2 us
    pallas_call x1, Pallas kernels, attention(): pl.pallas_call(attention_kernel, out_shape=(jax.ShapeDtypeStruct((blocks,...  5.14 us
  transfers between devices with their start and end apart: 5, of which 5 were waited for; matrix products, arithmetic and copies ran while one was open for 3% of the time, Pallas kernels for 4%

profile of v6, /device:TPU:1, one launch (start us, length us, event | category | flops | bytes accessed | tf_op | source)
XLA Modules:
  0.0 77.2 jit_solution(2513315881919892066)
XLA Ops:
  0.6 0.0 copy-start
  0.6 1.0 %copy-done = bf16[1,4,64,1024]{3,2,1,0:T(8,128)(2,1)S(1)} copy-done((bf16[1,4,64,1024]{3,2,1,0:T(8,128)(2,1)S(1)}, bf16[1,4,64,1024]{3,2,1,0:T(8,128)(2,1)}, u32[]{:S(2)}) %copy-start) | copy-done | bytes 524312
  1.7 0.0 copy-start.3
  1.7 0.0 copy-start.4
  1.7 0.1 rims.1
  1.7 5.7 %collective-permute-start = (bf16[2,64,1024]{2,1,0:T(8,128)(2,1)S(1)}, bf16[2,64,1024]{2,1,0:T(8,128)(2,1)S(1)}, u32[]{:S(2)}, u32[]{:S(2)}) collective-permute-start(bf16[2,64,1024]{2,1,0:T(8,128)(2,1)S(1)} %get-tuple-element.21), channel_id=1, source_target_pairs={{0,8},{1,9},{2,10},{3,11},{4,12},{5,13},{6,14},{7,15},{8,24},{9,25... | collective-permute-start | bytes 786440 | tf_op jit(solution)/shard_map/ppermute | solution.py:428
  7.4 1.9 %collective-permute-start.1 = (bf16[2,64,1024]{2,1,0:T(8,128)(2,1)S(1)}, bf16[2,64,1024]{2,1,0:T(8,128)(2,1)S(1)}, u32[]{:S(2)}, u32[]{:S(2)}) collective-permute-start(bf16[2,64,1024]{2,1,0:T(8,128)(2,1)S(1)} %get-tuple-element.22), channel_id=1, source_target_pairs={{0,16},{1,17},{2,18},{3,19},{4,20},{5,21},{6,22},{7,23},{8,0},{9,1... | collective-permute-start | bytes 786440 | tf_op jit(solution)/shard_map/ppermute | solution.py:429
  9.4 0.1 convert_element_type.12.u_ref
  9.5 0.0 copy-done.3
  9.6 0.0 copy-done.4
  9.6 1.0 %own_rows.1.known_ref = bf16[2,64,1024]{2,1,0:T(8,128)(2,1)S(1)} custom-call(f32[8]{0:T(128)S(1)} %sine_abs_fusion.c_ref, f32[4,64,1024]{2,1,0:T(8,128)S(1)} %convert_element_type.12.u_ref, f32[2,3,1024]{2,1,0:T(4,128)S(1)} %copy.9.one_ref), custom_call_target="tpu_custom_call" | custom-call | flops 2097152 | bytes 1048576 | tf_op jit(solution)/shard_map/own_rows/pallas_call | solution.py:124
  10.6 1.7 %fusion = (bf16[1024,256]{1,0:T(8,128)(2,1)S(1)}, bf16[1024,256]{1,0:T(8,128)(2,1)S(1)}, bf16[1024,256]{1,0:T(8,128)(2,1)S(1)}, bf16[1024,256]{1,0:T(8,128)(2,1)S(1)}) fusion(bf16[1024,1024]{1,0:T(8,128)(2,1)} %param.10), kind=kLoop, calls=%fused_computation.7 | loop fusion | bytes 4194304 | tf_op jit(solution)/shard_map/slice | solution.py:453
  12.3 0.0 copy-start.1
  12.3 0.0 copy-start.2
  12.3 6.0 %collective-permute-done.a_ref = bf16[2,64,1024]{2,1,0:T(8,128)(2,1)S(1)} collective-permute-done((bf16[2,64,1024]{2,1,0:T(8,128)(2,1)S(1)}, bf16[2,64,1024]{2,1,0:T(8,128)(2,1)S(1)}, u32[]{:S(2)}, u32[]{:S(2)}) %collective-permute-start) | collective-permute-done | bytes 262176 | tf_op jit(solution)/shard_map/ppermute | solution.py:428
  18.3 7.0 %collective-permute-done.1.b_ref = bf16[2,64,1024]{2,1,0:T(8,128)(2,1)S(1)} collective-permute-done((bf16[2,64,1024]{2,1,0:T(8,128)(2,1)S(1)}, bf16[2,64,1024]{2,1,0:T(8,128)(2,1)S(1)}, u32[]{:S(2)}, u32[]{:S(2)}) %collective-permute-start.1) | collective-permute-done | bytes 262176 | tf_op jit(solution)/shard_map/ppermute | solution.py:429
  25.4 0.1 pad_maximum_fusion
  25.4 3.5 %collective-permute-start.2 = (bf16[8,4,1024]{2,1,0:T(4,128)(2,1)S(1)}, bf16[8,4,1024]{2,1,0:T(4,128)(2,1)S(1)}, u32[]{:S(2)}, u32[]{:S(2)}) collective-permute-start(bf16[8,4,1024]{2,1,0:T(4,128)(2,1)S(1)} %pad_maximum_fusion), channel_id=1, source_target_pairs={{0,15},{1,0},{2,1},{3,2},{4,3},{5,4},{6,5},{7,6},{8,7},{9,8},{10,9... | collective-permute-start | bytes 196616 | tf_op jit(solution)/shard_map/ppermute | solution.py:435
  28.9 0.1 add_convert_fusion.flag_ref
  29.0 2.3 %inner.1 = (bf16[4,64,1024]{2,1,0:T(8,128)(2,1)S(1)}, bf16[8,8,1024]{2,1,0:T(8,128)(2,1)S(1)}) custom-call(f32[8]{0:T(128)S(1)} %sine_abs_fusion.c_ref, s32[3]{0:T(128)S(1)} %add_convert_fusion.flag_ref, f32[4,64,1024]{2,1,0:T(8,128)S(1)} %convert_element_type.12.u_ref, bf16[2,64,1024]{2,1,0:T(8,128)(2,1)S(1)} %own_rows.1.known_ref, ...), custom_call_target="tpu_custom_call" | custom-call | flops 10485760 | bytes 8388608 | tf_op jit(solution)/shard_map/inner/pallas_call | solution.py:182
  31.2 0.7 collective-permute-done.2.edge_ref
  31.9 0.0 copy-done.1
  31.9 0.0 copy-done.2
  31.9 2.9 %project.1 = (bf16[4,64,1024]{2,1,0:T(8,128)(2,1)S(1)}, bf16[4,4,64,384]{3,2,1,0:T(8,128)(2,1)}, bf16[4,16,1024]{2,1,0:T(8,128)(2,1)S(1)}) custom-call(f32[8]{0:T(128)S(1)} %sine_abs_fusion.c_ref, bf16[8,8,1024]{2,1,0:T(8,128)(2,1)S(1)} %get-tuple-element.23.side_ref, bf16[8,4,1024]{2,1,0:T(4,128)(2,1)S(1)} %collective-permute-done.2.edge_ref, ...), custom_call_target="tpu_custom_call" | custom-call | flops 805306368 | bytes 6291456 | tf_op jit(solution)/shard_map/project/pallas_call | solution.py:295
  34.9 6.9 %all-to-all-start = ((bf16[16,64,384]{2,1,0:T(8,128)(2,1)}), bf16[16,64,384]{2,1,0:T(8,128)(2,1)S(1)}, u32[]{:S(2)}, u32[]{:S(2)}) async-start(bf16[16,64,384]{2,1,0:T(8,128)(2,1)} %bitcast.5), calls=%async_computation | async-start | bytes 1572864 | tf_op jit(solution)/shard_map/all_to_all | solution.py:456
  41.8 3.5 %collective-permute-start.3 = (bf16[4,2,1024]{2,1,0:T(2,128)(2,1)S(1)}, bf16[4,2,1024]{2,1,0:T(2,128)(2,1)S(1)}, u32[]{:S(2)}, u32[]{:S(2)}) collective-permute-start(bf16[4,2,1024]{2,1,0:T(2,128)(2,1)S(1)} %slice.31), channel_id=1, source_target_pairs={{0,1},{1,2},{2,3},{3,4},{4,5},{5,6},{6,7},{7,8},{8,9},{9,10},{10,1... | collective-permute-start | bytes 49160 | tf_op jit(solution)/shard_map/ppermute | solution.py:457
  45.3 5.7 %collective-permute-done.3.displaced_ref = bf16[4,2,1024]{2,1,0:T(2,128)(2,1)S(1)} collective-permute-done((bf16[4,2,1024]{2,1,0:T(2,128)(2,1)S(1)}, bf16[4,2,1024]{2,1,0:T(2,128)(2,1)S(1)}, u32[]{:S(2)}, u32[]{:S(2)}) %collective-permute-start.3) | collective-permute-done | bytes 16416 | tf_op jit(solution)/shard_map/ppermute | solution.py:457
  51.1 5.2 %all-to-all-done = bf16[16,64,384]{2,1,0:T(8,128)(2,1)S(1)} async-done(((bf16[16,64,384]{2,1,0:T(8,128)(2,1)}), bf16[16,64,384]{2,1,0:T(8,128)(2,1)S(1)}, u32[]{:S(2)}, u32[]{:S(2)}) %all-to-all-start) | async-done | bytes 786464 | tf_op jit(solution)/shard_map/all_to_all | solution.py:456
  56.3 5.1 %attention.1 = (bf16[16,64,256]{2,1,0:T(8,128)(2,1)S(1)}, bf16[4,64,1024]{2,1,0:T(8,128)(2,1)}) custom-call(bf16[1024,384]{1,0:T(8,128)(2,1)S(1)} %bitcast.12, bf16[4,64,1024]{2,1,0:T(8,128)(2,1)S(1)} %get-tuple-element.28.mixed_ref), custom_call_target="tpu_custom_call" | custom-call | flops 1073741824 | bytes 1310720 | tf_op jit(solution)/shard_map/attention/pallas_call | solution.py:355
  61.4 14.9 %all_to_all.10.x_ref = bf16[16,64,256]{2,1,0:T(8,128)(2,1)S(1)} all-to-all(bf16[16,64,256]{2,1,0:T(8,128)(2,1)S(1)} %get-tuple-element.29), channel_id=1, replica_groups=mesh['lat'=32,'lon'=16] {'lon'}, dimensions={0} | all-to-all | bytes 1048576 | tf_op jit(solution)/shard_map/all_to_all | solution.py:462
  76.3 0.9 %gather_heads.1 = (bf16[4,64,1024]{2,1,0:T(8,128)(2,1)}, bf16[4,64,1024]{2,1,0:T(8,128)(2,1)}) custom-call(bf16[16,64,256]{2,1,0:T(8,128)(2,1)S(1)} %all_to_all.10.x_ref, bf16[4,16,1024]{2,1,0:T(8,128)(2,1)S(1)} %get-tuple-element.26.head_ref, bf16[4,2,1024]{2,1,0:T(2,128)(2,1)S(1)} %collective-permute-done.3.displaced_ref, ...), custom_call_target="tpu_custom_call", output_to_operand_aliasing={{1}: (3, {})} | custom-call | tf_op jit(solution)/shard_map/gather_heads/pallas_call | solution.py:401
  (7 shorter events, 0.1 us)
Async XLA Ops:
  0.6 1.0 %copy-start = (bf16[1,4,64,1024]{3,2,1,0:T(8,128)(2,1)S(1)}, bf16[1,4,64,1024]{3,2,1,0:T(8,128)(2,1)}, u32[]{:S(2)}) copy-start(bf16[1,4,64,1024]{3,2,1,0:T(8,128)(2,1)} %param.6) | copy-start | bytes 1572868
  1.7 7.9 %copy-start.3 = (f32[2,3,1024]{2,0,1:T(2,128)S(1)}, f32[2,3,1024]{2,0,1:T(2,128)}, u32[]{:S(2)}) copy-start(f32[2,3,1024]{2,0,1:T(2,128)} %param.7) | copy-start | bytes 73732
  1.7 7.9 %copy-start.4 = (f32[2,3,1024]{2,0,1:T(2,128)S(1)}, f32[2,3,1024]{2,0,1:T(2,128)}, u32[]{:S(2)}) copy-start(f32[2,3,1024]{2,0,1:T(2,128)} %param.8) | copy-start | bytes 73732
  1.7 16.6 %collective-permute-start = (bf16[2,64,1024]{2,1,0:T(8,128)(2,1)S(1)}, bf16[2,64,1024]{2,1,0:T(8,128)(2,1)S(1)}, u32[]{:S(2)}, u32[]{:S(2)}) collective-permute-start(bf16[2,64,1024]{2,1,0:T(8,128)(2,1)S(1)} %get-tuple-element.21), channel_id=1, source_target_pairs={{0,8},{1,9},{2,10},{3,11},{4,12},{5,13},{6,14},{7,15},{8,24},{9,25... | collective-permute-start | bytes 786440 | tf_op jit(solution)/shard_map/ppermute | solution.py:428
  7.4 17.9 %collective-permute-start.1 = (bf16[2,64,1024]{2,1,0:T(8,128)(2,1)S(1)}, bf16[2,64,1024]{2,1,0:T(8,128)(2,1)S(1)}, u32[]{:S(2)}, u32[]{:S(2)}) collective-permute-start(bf16[2,64,1024]{2,1,0:T(8,128)(2,1)S(1)} %get-tuple-element.22), channel_id=1, source_target_pairs={{0,16},{1,17},{2,18},{3,19},{4,20},{5,21},{6,22},{7,23},{8,0},{9,1... | collective-permute-start | bytes 786440 | tf_op jit(solution)/shard_map/ppermute | solution.py:429
  12.3 19.7 %copy-start.1 = (bf16[1024,512]{1,0:T(8,128)(2,1)S(1)}, bf16[1024,512]{1,0:T(8,128)(2,1)}, u32[]{:S(2)}) copy-start(bf16[1024,512]{1,0:T(8,128)(2,1)} %wkv.1) | copy-start | bytes 3145732
  12.3 19.7 %copy-start.2 = (f32[1024]{0:T(1024)S(1)}, f32[1024]{0:T(1024)}, u32[]{:S(2)}) copy-start(f32[1024]{0:T(1024)} %param.9) | copy-start | bytes 12292
  25.4 6.5 %collective-permute-start.2 = (bf16[8,4,1024]{2,1,0:T(4,128)(2,1)S(1)}, bf16[8,4,1024]{2,1,0:T(4,128)(2,1)S(1)}, u32[]{:S(2)}, u32[]{:S(2)}) collective-permute-start(bf16[8,4,1024]{2,1,0:T(4,128)(2,1)S(1)} %pad_maximum_fusion), channel_id=1, source_target_pairs={{0,15},{1,0},{2,1},{3,2},{4,3},{5,4},{6,5},{7,6},{8,7},{9,8},{10,9... | collective-permute-start | bytes 196616 | tf_op jit(solution)/shard_map/ppermute | solution.py:435
  34.9 21.4 %all-to-all-start = ((bf16[16,64,384]{2,1,0:T(8,128)(2,1)}), bf16[16,64,384]{2,1,0:T(8,128)(2,1)S(1)}, u32[]{:S(2)}, u32[]{:S(2)}) async-start(bf16[16,64,384]{2,1,0:T(8,128)(2,1)} %bitcast.5), calls=%async_computation | async-start | bytes 1572864 | tf_op jit(solution)/shard_map/all_to_all | solution.py:456
  41.8 9.3 %collective-permute-start.3 = (bf16[4,2,1024]{2,1,0:T(2,128)(2,1)S(1)}, bf16[4,2,1024]{2,1,0:T(2,128)(2,1)S(1)}, u32[]{:S(2)}, u32[]{:S(2)}) collective-permute-start(bf16[4,2,1024]{2,1,0:T(2,128)(2,1)S(1)} %slice.31), channel_id=1, source_target_pairs={{0,1},{1,2},{2,3},{3,4},{4,5},{5,6},{6,7},{7,8},{8,9},{9,10},{10,1... | collective-permute-start | bytes 49160 | tf_op jit(solution)/shard_map/ppermute | solution.py:457
